TPU v7x, 32 devices: a whole 2x2x4 slice. The times are simulated.
32 devices in a mesh: dp: 8 (over y, x, core), head: 4 (over z).
Axes of the slice: x: 2, y: 2, z: 4, core: 2. Of those that a mesh axis runs over, the one named last changes fastest.
Arguments:
- hidden_in: bfloat16 [2, 8192, 768], P(None, ('dp', 'head')), may hold values from -6 to 6
- teacher_in: bfloat16 [2, 8192, 768], P(None, ('dp', 'head')), may hold values from -6 to 6
- out_grad: bfloat16 [2, 8192, 768], P(None, ('dp', 'head')), may hold values from -6 to 6
- segment_ids: int32 [2, 16, 512], P(None, 'dp'), may hold values from 0 to 3, never falling along the last dimension, each value on 1 to 256 neighbouring positions
- qkv_latent: bfloat16 [3, 768, 768], P(None, None, 'head'), may hold values from -0.3125 to 0.3125
- out_latent: bfloat16 [768, 768], P('head'), may hold values from -0.875 to 0.875
- ffn_in_latent: bfloat16 [768, 3072], P(None, 'head'), may hold values from -0.21875 to 0.21875
- ffn_out_latent: bfloat16 [3072, 768], P('head'), may hold values from -0.109375 to 0.109375
- norm_gain: float32 [2, 768], replicated, may hold values from 0.5 to 1.5
- norm_bias: float32 [2, 768], replicated, may hold values from -2 to 2
- clips: float32 [4], replicated, may hold values from 0.75 to 2.5
- teacher_qkv: bfloat16 [3, 768, 768], P(None, None, 'head'), may hold values from -0.3125 to 0.3125
- teacher_out: bfloat16 [768, 768], P('head'), may hold values from -0.875 to 0.875
- teacher_ffn_in: bfloat16 [768, 3072], P(None, 'head'), may hold values from -0.21875 to 0.21875
- teacher_ffn_out: bfloat16 [3072, 768], P('head'), may hold values from -0.109375 to 0.109375
- teacher_gain: float32 [2, 768], replicated, may hold values from 0.5 to 1.5
- teacher_bias: float32 [2, 768], replicated, may hold values from -2 to 2
Outputs:
- hidden_out: bfloat16 [2, 8192, 768], P(None, ('dp', 'head'))
- hidden_in_grad: float32 [2, 8192, 768], P(None, ('dp', 'head'))
- qkv_grad: float32 [3, 768, 768], P(None, None, 'head')
- out_latent_grad: float32 [768, 768], P('head')
- ffn_in_grad: float32 [768, 3072], P(None, 'head')
- ffn_out_grad: float32 [3072, 768], P('head')
- gain_grad: float32 [2, 768], replicated
- bias_grad: float32 [2, 768], replicated
- clip_grad: float32 [4], replicated
Inputs may be any that keep to these rules, and one draw needn't show every extreme that they name: `segment_ids`: within each packed row of 512 tokens the documents are numbered in order from 0, never falling; attention stays within a document.
All inputs are finite; a program needn't handle non-finite values.
Results may differ from a plain program's by a relative error of at most 0.014.
Values may be sent and summed in bfloat16 or wider, within the bound.
No kernel may reach another device: no remote copies, remote signals or barrier semaphores. Data moves between devices by JAX's collectives and lax.ppermute only.
A program may use at most 128 MiB of HBM per device.

v0:
```python
import jax
import jax.numpy as jnp
from jax import lax
from jax.sharding import PartitionSpec as P

D = 768
HD = 64
FF = 3072
SEQ = 512
MICRO = 2


def soft_clip(values, clip_level):
    return clip_level * jnp.tanh(values / clip_level)


def clip_back(upstream, values, clip_level):
    tangent = jnp.tanh(values / clip_level)
    clip_slope = 1.0 - tangent * tangent
    return (upstream * clip_slope, jnp.sum(upstream * (tangent - values / clip_level * clip_slope)))


def norm_fwd(values, gain_vec, shift_vec):
    centred = values - jnp.mean(values, axis=-1, keepdims=True)
    inv_std = lax.rsqrt(jnp.mean(centred * centred, axis=-1, keepdims=True) + 1e-06)
    normed = centred * inv_std
    return (normed * gain_vec + shift_vec, normed, inv_std)


def norm_back(upstream, normed, inv_std, gain_vec):
    scaled = upstream * gain_vec
    centred_grad = (
        scaled
        - jnp.mean(scaled, axis=-1, keepdims=True)
        - normed * jnp.mean(scaled * normed, axis=-1, keepdims=True)
    )
    return (centred_grad * inv_std, jnp.sum(upstream * normed, axis=0), jnp.sum(upstream, axis=0))


def gelu_exact(values):
    return jax.nn.gelu(values, approximate=False)


def gelu_slope(values):
    normal_cdf = 0.5 * (1.0 + lax.erf(values * 0.7071067811865476))
    density = jnp.exp(-0.5 * values * values) * 0.3989422804014327
    return normal_cdf + values * density


def matmul_nt(left_op, right_op):
    return lax.dot_general(
        left_op, right_op, (((1,), (1,)), ((), ())), preferred_element_type=jnp.float32
    )


def matmul_tn(left_op, right_op):
    return lax.dot_general(
        left_op, right_op, (((0,), (0,)), ((), ())), preferred_element_type=jnp.float32
    )


def masked_scores(queries, key_rows, segment_row):
    scores = (
        jnp.einsum("qhd,khd->hqk", queries, key_rows, preferred_element_type=jnp.float32) * 0.125
    )
    same_segment = segment_row[:, None] == segment_row[None, :]
    return (jnp.where(same_segment[None], scores, -1000000000.0), same_segment)


def attend_rows(operands):
    student, teacher, segment_row = operands
    scores, same_segment = masked_scores(student[:, 0], student[:, 1], segment_row)
    row_peak = jnp.max(scores, axis=-1, keepdims=True)
    powers = jnp.exp(scores - row_peak)
    row_total = jnp.sum(powers, axis=-1, keepdims=True)
    soft_weights = powers / row_total
    context = jnp.einsum(
        "hqk,khd->qhd",
        soft_weights.astype(jnp.bfloat16),
        student[:, 2],
        preferred_element_type=jnp.float32,
    )
    t_scores, unused_mask = masked_scores(teacher[:, 0], teacher[:, 1], segment_row)
    t_weights = jax.nn.softmax(t_scores, axis=-1)
    t_context = jnp.einsum(
        "hqk,khd->qhd",
        t_weights.astype(jnp.bfloat16),
        teacher[:, 2],
        preferred_element_type=jnp.float32,
    )
    return (context, (row_peak + jnp.log(row_total))[..., 0], t_context.astype(jnp.bfloat16))


def attend_back(operands):
    student, teacher, log_total, grad_ctx, segment_row = operands
    scores, same_segment = masked_scores(student[:, 0], student[:, 1], segment_row)
    soft_weights = jnp.exp(scores - log_total[..., None])
    grad_weights = jnp.einsum(
        "qhd,khd->hqk", grad_ctx, student[:, 2], preferred_element_type=jnp.float32
    )
    grad_values = jnp.einsum(
        "hqk,qhd->khd",
        soft_weights.astype(jnp.bfloat16),
        grad_ctx,
        preferred_element_type=jnp.float32,
    )
    t_scores, unused_mask = masked_scores(teacher[:, 0], teacher[:, 1], segment_row)
    weight_sum = jnp.sum(soft_weights * grad_weights, axis=-1, keepdims=True)
    seq_len = scores.shape[-1]
    grad_scores = (
        soft_weights * (grad_weights - weight_sum)
        + jnp.where(same_segment[None], scores - t_scores, 0.0) / seq_len
    )
    grad_scores = grad_scores.astype(jnp.bfloat16)
    grad_queries = (
        jnp.einsum("hqk,khd->qhd", grad_scores, student[:, 1], preferred_element_type=jnp.float32)
        * 0.125
    )
    grad_keys = (
        jnp.einsum("hqk,qhd->khd", grad_scores, student[:, 0], preferred_element_type=jnp.float32)
        * 0.125
    )
    return jnp.stack([grad_queries, grad_keys, grad_values], axis=1).astype(jnp.bfloat16)


def binarize_factors(latent, level):
    scaled_unit = 2.0 * latent / level
    tangent = jnp.tanh(scaled_unit)
    slope_sq = 1.0 - tangent * tangent
    return (
        (level * tangent).astype(jnp.bfloat16),
        2.0 * slope_sq,
        tangent - scaled_unit * slope_sq,
    )


def on_device(
    hidden_in,
    teacher_in,
    out_grad,
    segment_ids,
    qkv_latent,
    out_latent,
    ffn_in_latent,
    ffn_out_latent,
    norm_gain,
    norm_bias,
    clips,
    teacher_qkv,
    teacher_out,
    teacher_ffn_in,
    teacher_ffn_out,
    teacher_gain,
    teacher_bias,
):
    latents = [
        qkv_latent[0].astype(jnp.float32),
        qkv_latent[1].astype(jnp.float32),
        qkv_latent[2].astype(jnp.float32),
        out_latent.astype(jnp.float32),
        ffn_in_latent.astype(jnp.float32),
        ffn_out_latent.astype(jnp.float32),
    ]
    squares = jnp.stack([jnp.sum(latent_item * latent_item) for latent_item in latents])
    totals = lax.psum(squares, "head")
    entries = jnp.array([D * D, D * D, D * D, D * D, D * FF, FF * D], jnp.float32)
    rms_all = jnp.sqrt(totals / entries + 1e-06)
    factors = [binarize_factors(latents[position], rms_all[position]) for position in range(6)]
    qkv_bin = jnp.stack([factors[position][0] for position in range(3)])
    out_bin = factors[3][0]
    ffn_in_bin = factors[4][0]
    ffn_out_bin = factors[5][0]
    heads_local = qkv_latent.shape[-1] // HD

    def to_latent(bin_grads):
        return tuple((bin_grads[position] * factors[position][1] for position in range(6)))

    grad_bins = [jnp.zeros_like(latent_item) for latent_item in latents]
    direct_acc = [jnp.zeros_like(latent_item) for latent_item in latents]
    gain_acc = jnp.zeros((2, hidden_in.shape[-1]), jnp.float32)
    bias_acc = jnp.zeros((2, hidden_in.shape[-1]), jnp.float32)
    clip_acc = jnp.zeros((4,), jnp.float32)
    outputs = []
    input_grads = []
    for micro_index in range(MICRO):
        x_vals = hidden_in[micro_index].astype(jnp.float32)
        t_vals = teacher_in[micro_index]
        x_quant = soft_clip(x_vals, clips[0]).astype(jnp.bfloat16)
        student_rows, teacher_rows = lax.all_gather((x_quant, t_vals), "head", axis=0, tiled=True)
        student_qkv = jnp.einsum(
            "nd,jde->nje", student_rows, qkv_bin, preferred_element_type=jnp.float32
        ).astype(jnp.bfloat16)
        teacher_proj = jnp.einsum(
            "nd,jde->nje", teacher_rows, teacher_qkv, preferred_element_type=jnp.float32
        ).astype(jnp.bfloat16)
        tokens = student_rows.shape[0]
        row_count = tokens // SEQ
        qkv_rows = student_qkv.reshape(row_count, SEQ, 3, heads_local, HD)
        t_rows = teacher_proj.reshape(row_count, SEQ, 3, heads_local, HD)
        seg_rows = segment_ids[micro_index]
        context, log_total, t_context = lax.map(attend_rows, (qkv_rows, t_rows, seg_rows))
        context = context.reshape(tokens, -1)
        t_context = t_context.reshape(tokens, -1)
        ctx_quant = soft_clip(context, clips[1]).astype(jnp.bfloat16)
        attn_s, attn_t = (
            lax.psum_scatter(
                jnp.dot(ctx_quant, out_bin, preferred_element_type=jnp.float32).astype(
                    jnp.bfloat16
                ),
                "head",
                scatter_dimension=0,
                tiled=True,
            ).astype(jnp.float32),
            lax.psum_scatter(
                jnp.dot(t_context, teacher_out, preferred_element_type=jnp.float32).astype(
                    jnp.bfloat16
                ),
                "head",
                scatter_dimension=0,
                tiled=True,
            ).astype(jnp.float32),
        )
        t_input = t_vals.astype(jnp.float32)
        first_norm, normed_one, inv_one = norm_fwd(x_vals + attn_s, norm_gain[0], norm_bias[0])
        t_first = norm_fwd(t_input + attn_t, teacher_gain[0], teacher_bias[0])[0]
        first_quant = soft_clip(first_norm, clips[2]).astype(jnp.bfloat16)
        project_student_rows, project_teacher_rows = lax.all_gather(
            (first_quant, t_first.astype(jnp.bfloat16)), "head", axis=0, tiled=True
        )
        student_pre = jnp.dot(project_student_rows, ffn_in_bin, preferred_element_type=jnp.float32)
        teacher_act = gelu_exact(
            jnp.dot(project_teacher_rows, teacher_ffn_in, preferred_element_type=jnp.float32)
        ).astype(jnp.bfloat16)
        activation = gelu_exact(student_pre)
        hidden_quant = soft_clip(activation, clips[3]).astype(jnp.bfloat16)
        ffn_s, ffn_t = (
            lax.psum_scatter(
                jnp.dot(hidden_quant, ffn_out_bin, preferred_element_type=jnp.float32).astype(
                    jnp.bfloat16
                ),
                "head",
                scatter_dimension=0,
                tiled=True,
            ).astype(jnp.float32),
            lax.psum_scatter(
                jnp.dot(teacher_act, teacher_ffn_out, preferred_element_type=jnp.float32).astype(
                    jnp.bfloat16
                ),
                "head",
                scatter_dimension=0,
                tiled=True,
            ).astype(jnp.float32),
        )
        result, normed_two, inv_two = norm_fwd(first_norm + ffn_s, norm_gain[1], norm_bias[1])
        t_result = norm_fwd(t_first + ffn_t, teacher_gain[1], teacher_bias[1])[0]
        outputs.append(result.astype(jnp.bfloat16))
        grad_result = out_grad[micro_index].astype(jnp.float32) + result - t_result
        grad_pre2, gain_two, bias_two = norm_back(grad_result, normed_two, inv_two, norm_gain[1])
        rows_piece = lax.all_gather(grad_pre2.astype(jnp.bfloat16), "head", axis=0, tiled=True)
        grad_hq = matmul_nt(rows_piece, ffn_out_bin)
        grad_ffn_out = matmul_tn(hidden_quant, rows_piece)
        grad_act, clip_three = clip_back(grad_hq, activation, clips[3])
        grad_hidden = (grad_act * gelu_slope(student_pre)).astype(jnp.bfloat16)
        grad_ffn_in = matmul_tn(project_student_rows, grad_hidden)
        grad_fq = lax.psum_scatter(
            matmul_nt(grad_hidden, ffn_in_bin).astype(jnp.bfloat16),
            "head",
            scatter_dimension=0,
            tiled=True,
        ).astype(jnp.float32)
        grad_first, clip_two = clip_back(grad_fq, first_norm, clips[2])
        grad_pre1, gain_one, bias_one = norm_back(
            grad_first + grad_pre2, normed_one, inv_one, norm_gain[0]
        )
        attn_rows_piece = lax.all_gather(grad_pre1.astype(jnp.bfloat16), "head", axis=0, tiled=True)
        grad_cq = matmul_nt(attn_rows_piece, out_bin)
        grad_out_w = matmul_tn(ctx_quant, attn_rows_piece)
        grad_ctx, clip_one = clip_back(grad_cq, context, clips[1])
        grad_ctx_rows = grad_ctx.astype(jnp.bfloat16).reshape(row_count, SEQ, heads_local, HD)
        grad_qkv = lax.map(
            attend_back, (qkv_rows, t_rows, log_total, grad_ctx_rows, seg_rows)
        ).reshape(tokens, 3, -1)
        grad_qkv_w = jnp.einsum(
            "nd,nje->jde", student_rows, grad_qkv, preferred_element_type=jnp.float32
        )
        grad_xq = lax.psum_scatter(
            jnp.einsum("nje,jde->nd", grad_qkv, qkv_bin, preferred_element_type=jnp.float32).astype(
                jnp.bfloat16
            ),
            "head",
            scatter_dimension=0,
            tiled=True,
        ).astype(jnp.float32)
        grad_input, clip_zero = clip_back(grad_xq, x_vals, clips[0])
        input_grads.append(grad_input + grad_pre1)
        gain_acc = gain_acc + jnp.stack([gain_one, gain_two])
        bias_acc = bias_acc + jnp.stack([bias_one, bias_two])
        clip_acc = clip_acc + jnp.stack([clip_zero, clip_one, clip_two, clip_three])
        micro_bins = [
            grad_qkv_w[0],
            grad_qkv_w[1],
            grad_qkv_w[2],
            grad_out_w,
            grad_ffn_in,
            grad_ffn_out,
        ]
        grad_bins = [grad_bins[position] + micro_bins[position] for position in range(6)]
    direct_acc = list(lax.psum(to_latent(grad_bins), "dp"))
    rms_local = jnp.stack(
        [jnp.sum(grad_bins[position] * factors[position][2]) for position in range(6)]
    )
    rms_sum, gain_grad, bias_grad, clip_grad = lax.psum(
        (rms_local, gain_acc, bias_acc, clip_acc), ("dp", "head")
    )
    finals = [
        direct_acc[position]
        + rms_sum[position] * latents[position] / (entries[position] * rms_all[position])
        for position in range(6)
    ]
    qkv_grad = jnp.stack(finals[:3])
    return (
        jnp.stack(outputs),
        jnp.stack(input_grads),
        qkv_grad,
        finals[3],
        finals[4],
        finals[5],
        gain_grad,
        bias_grad,
        clip_grad,
    )


def solution(mesh):
    placed = (
        P(None, ("dp", "head"), None),
        P(None, ("dp", "head"), None),
        P(None, ("dp", "head"), None),
        P(None, "dp", None),
        P(None, None, "head"),
        P("head", None),
        P(None, "head"),
        P("head", None),
        P(),
        P(),
        P(),
        P(None, None, "head"),
        P("head", None),
        P(None, "head"),
        P("head", None),
        P(),
        P(),
    )
    return jax.shard_map(
        on_device,
        mesh=mesh,
        in_specs=placed,
        out_specs=(
            P(None, ("dp", "head"), None),
            P(None, ("dp", "head"), None),
            P(None, None, "head"),
            P("head", None),
            P(None, "head"),
            P("head", None),
            P(),
            P(),
            P(),
        ),
        check_vma=False,
    )
```

profile of v0, /device:TPU:0, one launch (start us, length us, event | category | flops | bytes accessed | tf_op | source)
XLA Modules:
  0.0 1148.5 jit_solution(1805911072511009720)
XLA Ops:
  23.4 13.8 %psum.77 = f32[6]{0:T(128)S(1)} all-reduce(f32[6]{0:T(128)S(1)} %stack.174), channel_id=1, replica_groups=mesh['dp'=8,'head'=4] {'head'}, use_global_device_ids=true, to_apply=%region_6.0 | all-reduce | flops 6 | bytes 48 | tf_op jit(solution)/shard_map/psum | solution.py:165
  41.7 8.6 all-gather.35.cloned.1.call-done
  55.1 33.3 %all-gather.37.cloned.1.call-done = bf16[1,1024,768]{2,1,0:T(8,128)(2,1)} async-done(((bf16[1,256,768]{2,1,0:T(8,128)(2,1)}), bf16[1,1024,768]{2,1,0:T(8,128)(2,1)}) %all-gather.37.cloned.1.call-update) | async-done | bytes 1572880 | tf_op jit(solution)/shard_map/all_gather | solution.py:189
  93.5 33.0 %all-gather.19.cloned.1.call-done = bf16[1024,768]{1,0:T(8,128)(2,1)} async-done(((bf16[256,768]{1,0:T(8,128)(2,1)}), bf16[1024,768]{1,0:T(8,128)(2,1)}) %all-gather.19.cloned.1.call-update) | async-done | bytes 1572880 | tf_op jit(solution)/shard_map/all_gather | solution.py:189
  131.6 32.9 %all-gather.15.cloned.1.call-done = bf16[1024,768]{1,0:T(8,128)(2,1)} async-done(((bf16[256,768]{1,0:T(8,128)(2,1)}), bf16[1024,768]{1,0:T(8,128)(2,1)}) %all-gather.15.cloned.1.call-update) | async-done | bytes 1572880 | tf_op jit(solution)/shard_map/all_gather | solution.py:189
  169.9 18.9 %while.48 = (s32[]{:T(128)}, f32[2,512,3,64]{1,3,2,0:T(8,128)S(1)}, f32[2,3,512]{2,1,0:T(4,128)S(1)}, bf16[2,512,3,64]{1,3,2,0:T(8,128)(2,1)S(1)}, bf16[2,512,3,...) while((s32[]{:T(128)}, f32[2,512,3,64]{1,3,2,0:T(8,128)S(1)}, ...), condition=%wide.region_12.13_spmd, body=%wide.region_7.12_spmd.sunk | while | flops 417168384 | bytes 21248112 | solution.py:201
  191.7 19.0 %while.49 = (s32[]{:T(128)}, f32[2,512,3,64]{1,3,2,0:T(8,128)S(1)}, f32[2,3,512]{2,1,0:T(4,128)S(1)}, bf16[2,512,3,64]{1,3,2,0:T(8,128)(2,1)S(1)}, bf16[2,512,3,...) while((s32[]{:T(128)}, f32[2,512,3,64]{1,3,2,0:T(8,128)S(1)}, ...), condition=%wide.region_24.25_spmd, body=%wide.region_19.24_spmd.sunk | while | flops 417168384 | bytes 21248112 | solution.py:201
  226.6 35.8 %reduce-scatter.29.cloned.1.call-done = bf16[256,768]{1,0:T(8,128)(2,1)} async-done(((bf16[1024,768]{1,0:T(8,128)(2,1)}), bf16[256,768]{1,0:T(8,128)(2,1)}) %reduce-scatter.29.cloned.1.call-update) | async-done | bytes 393232 | tf_op jit(solution)/shard_map/reduce_scatter | solution.py:214
  267.5 32.2 %reduce-scatter.13.cloned.1.call-done = bf16[256,768]{1,0:T(8,128)(2,1)} async-done(((bf16[1024,768]{1,0:T(8,128)(2,1)}), bf16[256,768]{1,0:T(8,128)(2,1)}) %reduce-scatter.13.cloned.1.call-update) | async-done | bytes 393232 | tf_op jit(solution)/shard_map/reduce_scatter | solution.py:206
  299.6 37.2 %reduce-scatter.17.cloned.1.call-done = bf16[256,768]{1,0:T(8,128)(2,1)} async-done(((bf16[1024,768]{1,0:T(8,128)(2,1)}), bf16[256,768]{1,0:T(8,128)(2,1)}) %reduce-scatter.17.cloned.1.call-update) | async-done | bytes 393232 | tf_op jit(solution)/shard_map/reduce_scatter | solution.py:206
  342.3 32.7 %all-gather.23.cloned.1.call-done = bf16[1024,768]{1,0:T(8,128)(2,1)} async-done(((bf16[256,768]{1,0:T(8,128)(2,1)}), bf16[1024,768]{1,0:T(8,128)(2,1)}) %all-gather.23.cloned.1.call-update) | async-done | bytes 1572880 | tf_op jit(solution)/shard_map/all_gather | solution.py:227
  375.0 11.5 %convolution_convert_fusion.4 = bf16[1024,768]{1,0:T(8,128)(2,1)} fusion(bf16[768,768]{1,0:T(8,128)(2,1)S(1)} %copy-done, bf16[1024,768]{1,0:T(8,128)(2,1)} %all-gather.23.cloned.1.call-done, bf16[768,768]{1,0:T(8,128)(2,1)} %param.39), kind=kOutput, calls=%fused_computation.325 | convolution fusion | flops 2467823616 | bytes 5505024 | tf_op jit(solution)/shard_map/dot_general | solution.py:246
  386.6 26.4 %all-gather.17.cloned.1.call-done = bf16[1024,768]{1,0:T(8,128)(2,1)} async-done(((bf16[256,768]{1,0:T(8,128)(2,1)}), bf16[1024,768]{1,0:T(8,128)(2,1)}) %all-gather.17.cloned.1.call-update) | async-done | bytes 1572880 | tf_op jit(solution)/shard_map/all_gather | solution.py:227
  413.0 23.8 %fusion.208 = (f32[1024,768]{1,0:T(8,128)S(1)}, f32[1024,768]{1,0:T(8,128)}) fusion(f32[]{:T(128)} %bitcast.82, bf16[1024,768]{1,0:T(8,128)(2,1)} %all-gather.17.cloned.1.call-done, f32[]{:T(128)} %bitcast.84, bf16[768,768]{1,0:T(8,128)(2,1)} %param.32), kind=kOutput, calls=%fused_computation.212 | convolution fusion | flops 1262026752 | bytes 9043976 | tf_op jit(solution)/shard_map/dot_general | solution.py:230
  443.8 6.2 reduce-scatter.23.cloned.1.call-done
  454.9 32.2 %reduce-scatter.15.cloned.1.call-done = bf16[256,768]{1,0:T(8,128)(2,1)} async-done(((bf16[1024,768]{1,0:T(8,128)(2,1)}), bf16[256,768]{1,0:T(8,128)(2,1)}) %reduce-scatter.15.cloned.1.call-update) | async-done | bytes 393232 | tf_op jit(solution)/shard_map/reduce_scatter | solution.py:237
  490.9 34.4 %all-gather.29.cloned.1.call-done = bf16[1024,768]{1,0:T(8,128)(2,1)} async-done(((bf16[256,768]{1,0:T(8,128)(2,1)}), bf16[1024,768]{1,0:T(8,128)(2,1)}) %all-gather.29.cloned.1.call-update) | async-done | bytes 1572880 | tf_op jit(solution)/shard_map/all_gather | solution.py:227
  525.3 11.5 %convolution_convert_fusion.1 = bf16[1024,768]{1,0:T(8,128)(2,1)} fusion(bf16[768,768]{1,0:T(8,128)(2,1)S(1)} %copy-done, bf16[1024,768]{1,0:T(8,128)(2,1)} %all-gather.29.cloned.1.call-done, bf16[768,768]{1,0:T(8,128)(2,1)} %param.39), kind=kOutput, calls=%fused_computation.322 | convolution fusion | flops 2467823616 | bytes 5505024 | tf_op jit(solution)/shard_map/dot_general | solution.py:246
  536.9 26.4 %all-gather.21.cloned.1.call-done = bf16[1024,768]{1,0:T(8,128)(2,1)} async-done(((bf16[256,768]{1,0:T(8,128)(2,1)}), bf16[1024,768]{1,0:T(8,128)(2,1)}) %all-gather.21.cloned.1.call-update) | async-done | bytes 1572880 | tf_op jit(solution)/shard_map/all_gather | solution.py:227
  563.3 23.7 %fusion.211 = (f32[1024,768]{1,0:T(8,128)S(1)}, f32[1024,768]{1,0:T(8,128)}) fusion(f32[]{:T(128)} %bitcast.82, bf16[1024,768]{1,0:T(8,128)(2,1)} %all-gather.21.cloned.1.call-done, f32[]{:T(128)} %bitcast.84, bf16[768,768]{1,0:T(8,128)(2,1)} %param.32), kind=kOutput, calls=%fused_computation.215 | convolution fusion | flops 1262026752 | bytes 9043976 | tf_op jit(solution)/shard_map/dot_general | solution.py:230
  588.7 5.3 convolution_convert_fusion.6
  602.7 34.5 %reduce-scatter.19.cloned.1.call-done = bf16[256,768]{1,0:T(8,128)(2,1)} async-done(((bf16[1024,768]{1,0:T(8,128)(2,1)}), bf16[256,768]{1,0:T(8,128)(2,1)}) %reduce-scatter.19.cloned.1.call-update) | async-done | bytes 393232 | tf_op jit(solution)/shard_map/reduce_scatter | solution.py:237
  644.9 35.6 %all-gather.25.cloned.1.call-done = bf16[1024,768]{1,0:T(8,128)(2,1)} async-done(((bf16[256,768]{1,0:T(8,128)(2,1)}), bf16[1024,768]{1,0:T(8,128)(2,1)}) %all-gather.25.cloned.1.call-update) | async-done | bytes 1572880 | tf_op jit(solution)/shard_map/all_gather | solution.py:259
  680.5 8.2 multiply_reduce_fusion.3
  693.2 25.2 %all-gather.31.cloned.1.call-done = bf16[1024,768]{1,0:T(8,128)(2,1)} async-done(((bf16[256,768]{1,0:T(8,128)(2,1)}), bf16[1024,768]{1,0:T(8,128)(2,1)}) %all-gather.31.cloned.1.call-update) | async-done | bytes 1572880 | tf_op jit(solution)/shard_map/all_gather | solution.py:259
  718.5 7.2 multiply_reduce_fusion.2
  730.2 25.3 %reduce-scatter.25.cloned.1.call-done = bf16[256,768]{1,0:T(8,128)(2,1)} async-done(((bf16[1024,768]{1,0:T(8,128)(2,1)}), bf16[256,768]{1,0:T(8,128)(2,1)}) %reduce-scatter.25.cloned.1.call-update) | async-done | bytes 393232 | tf_op jit(solution)/shard_map/reduce_scatter | solution.py:265
  755.5 37.0 %reduce-scatter.33.cloned.1.call-done = bf16[256,768]{1,0:T(8,128)(2,1)} async-done(((bf16[1024,768]{1,0:T(8,128)(2,1)}), bf16[256,768]{1,0:T(8,128)(2,1)}) %reduce-scatter.33.cloned.1.call-update) | async-done | bytes 393232 | tf_op jit(solution)/shard_map/reduce_scatter | solution.py:265
  804.9 5.0 multiply_reduce_fusion.5
  810.0 27.3 %all-gather.33.cloned.1.call-done = bf16[1024,768]{1,0:T(8,128)(2,1)} async-done(((bf16[256,768]{1,0:T(8,128)(2,1)}), bf16[1024,768]{1,0:T(8,128)(2,1)}) %all-gather.33.cloned.1.call-update) | async-done | bytes 1572880 | tf_op jit(solution)/shard_map/all_gather | solution.py:275
  842.9 57.3 %while.51 = (s32[]{:T(128)}, bf16[2,512,3,3,64]{1,4,3,2,0:T(8,128)(2,1)}, bf16[2,512,3,3,64]{1,4,3,2,0:T(8,128)(2,1)}, s32[2,512]{1,0:T(2,128)S(1)}, f32[2,3,512...) while((s32[]{:T(128)}, ...), condition=%wide.region_59.60_spmd, body=%wide.region_57.59_spmd.sunk | while | flops 634818560 | bytes 55503020 | solution.py:280
  853.3 8.2 fusion.556
  861.4 8.2 fusion.555
  881.9 8.2 fusion.556
  890.1 8.2 fusion.555
  912.6 57.3 %while.50 = (s32[]{:T(128)}, bf16[2,512,3,3,64]{1,4,3,2,0:T(8,128)(2,1)}, bf16[2,512,3,3,64]{1,4,3,2,0:T(8,128)(2,1)}, s32[2,512]{1,0:T(2,128)S(1)}, f32[2,3,512...) while((s32[]{:T(128)}, ...), condition=%wide.region_44.45_spmd, body=%wide.region_42.44_spmd.sunk | while | flops 634818560 | bytes 55503020 | solution.py:280
  923.0 8.2 fusion.545
  931.1 8.2 fusion.544
  951.6 8.2 fusion.545
  959.8 8.2 fusion.544
  976.3 5.1 fusion.347
  981.5 5.7 multiply_reduce_fusion.4
  1011.5 4.5 stack.188
  1016.0 4.3 fusion.293
  1020.3 5.0 maximum_add_fusion.2
  1026.3 40.8 %all-reduce = (f32[6]{0:T(128)S(1)}, f32[2,768]{1,0:T(2,128)}, f32[2,768]{1,0:T(2,128)}, f32[4]{0:T(128)}) all-reduce(f32[6]{0:T(128)} %stack.188, f32[2,768]{1,0:T(2,128)} %maximum_add_fusion, f32[2,768]{1,0:T(2,128)} %maximum_add_fusion.1, f32[4]{0:T(128)S(1)} %maximum_add_fusion.2), channel_id=1, replica_groups=mesh['dp'=8,'head'=4] {'dp','head'}, use_global_device_ids=true, to_apply=%region_68.69 | all-reduce | flops 3082 | bytes 24656 | tf_op jit(solution)/shard_map/psum | solution.py:312
  1071.3 58.4 %all-reduce.4.cloned.1.call-done = (f32[768,192]{0,1:T(8,128)}, f32[768,192]{0,1:T(8,128)}, f32[768,192]{0,1:T(8,128)}, f32[192,768]{1,0:T(8,128)}, f32[768,768]{1,0:T(8,128)}, /*index=5*/f32[768,768]{1,0:T(8,128)}) async-done(((f32[768,192]{0,1:T(8,128)}, f32[768,192]{0,1:T(8,128)}, f32[768,192]{0,1:T(8,128)}, f32[192,768]{1,0:T(8,128)}, f32[768,768]{1,0:T(8,128)}, /*index=5*/f32[768,768]{1,0:T(8,128)}), ...) | async-done | bytes 7077904 | tf_op jit(solution)/shard_map/psum | solution.py:308
  1129.7 4.4 fusion.265
  (517 shorter events, 268.5 us)
Async XLA Ops:
  7.2 367.9 %copy-start = (bf16[768,768]{1,0:T(8,128)(2,1)S(1)}, bf16[768,768]{1,0:T(8,128)(2,1)}, u32[]{:S(2)}) copy-start(bf16[768,768]{1,0:T(8,128)(2,1)} %param.40) | copy-start | bytes 3538948
  7.2 43.1 %all-gather.35.cloned.1.call-start = ((), (), s32[]{:S(2)}) async-start(), calls=%async_computation.34 | async-start | bytes 1966080 | tf_op jit(solution)/shard_map/all_gather | solution.py:189
  9.5 78.9 %all-gather.37.cloned.1.call-start = ((), (), s32[]{:S(2)}) async-start(), calls=%async_computation.35 | async-start | bytes 1966080 | tf_op jit(solution)/shard_map/all_gather | solution.py:189
  10.2 116.3 %all-gather.19.cloned.1.call-start = ((), (), s32[]{:S(2)}) async-start(), calls=%async_computation.16 | async-start | bytes 1966080 | tf_op jit(solution)/shard_map/all_gather | solution.py:189
  14.7 149.9 %all-gather.15.cloned.1.call-start = ((), (), s32[]{:S(2)}) async-start(), calls=%async_computation.12 | async-start | bytes 1966080 | tf_op jit(solution)/shard_map/all_gather | solution.py:189
  15.3 210.1 %reduce-scatter.21.cloned.1.call-start = ((), (), s32[]{:S(2)}) async-start(), calls=%async_computation.20 | async-start | bytes 1966080 | tf_op jit(solution)/shard_map/reduce_scatter | solution.py:214
  191.1 71.3 %reduce-scatter.29.cloned.1.call-start = ((), (), s32[]{:S(2)}) async-start(), calls=%async_computation.27 | async-start | bytes 1966080 | tf_op jit(solution)/shard_map/reduce_scatter | solution.py:214
  212.9 86.7 %reduce-scatter.13.cloned.1.call-start = ((), (), s32[]{:S(2)}) async-start(), calls=%async_computation.13 | async-start | bytes 1966080 | tf_op jit(solution)/shard_map/reduce_scatter | solution.py:206
  218.7 118.1 %reduce-scatter.17.cloned.1.call-start = ((), (), s32[]{:S(2)}) async-start(), calls=%async_computation.17 | async-start | bytes 1966080 | tf_op jit(solution)/shard_map/reduce_scatter | solution.py:206
  224.6 42.2 %copy-start.108 = (f32[2,768]{1,0:T(2,128)S(1)}, f32[2,768]{1,0:T(2,128)}, u32[]{:S(2)}) copy-start(f32[2,768]{1,0:T(2,128)} %param.35) | copy-start | bytes 18436
  224.6 42.2 %copy-start.109 = (f32[2,768]{1,0:T(2,128)S(1)}, f32[2,768]{1,0:T(2,128)}, u32[]{:S(2)}) copy-start(f32[2,768]{1,0:T(2,128)} %param.34) | copy-start | bytes 18436
  224.6 112.2 %copy-start.2 = (bf16[2,256,768]{2,1,0:T(8,128)(2,1)S(1)}, bf16[2,256,768]{2,1,0:T(8,128)(2,1)}, u32[]{:S(2)}) copy-start(bf16[2,256,768]{2,1,0:T(8,128)(2,1)} %param.26) | copy-start | bytes 2359300
  224.6 150.4 %all-gather.23.cloned.1.call-start = ((), (), s32[]{:S(2)}) async-start(), calls=%async_computation.21 | async-start | bytes 1966080 | tf_op jit(solution)/shard_map/all_gather | solution.py:227
  225.3 112.9 %copy-start.87 = (f32[768]{0:T(1024)}, f32[768]{0:T(1024)S(1)}, u32[]{:S(2)}) copy-start(f32[768]{0:T(1024)S(1)} %get-tuple-element.261) | copy-start | bytes 9220
  225.3 112.9 %copy-start.88 = (f32[768]{0:T(1024)}, f32[768]{0:T(1024)S(1)}, u32[]{:S(2)}) copy-start(f32[768]{0:T(1024)S(1)} %get-tuple-element.438) | copy-start | bytes 9220
  226.6 113.7 %copy-start.95 = (f32[256]{0:T(256)}, f32[256]{0:T(256)S(1)}, u32[]{:S(2)}) copy-start(f32[256]{0:T(256)S(1)} %broadcast_multiply_fusion.11) | copy-start | bytes 3076
  263.9 78.2 %copy-start.94 = (f32[256]{0:T(256)}, f32[256]{0:T(256)S(1)}, u32[]{:S(2)}) copy-start(f32[256]{0:T(256)S(1)} %get-tuple-element.437) | copy-start | bytes 3076
  263.9 78.2 %copy-start.102 = (f32[256]{0:T(256)}, f32[256]{0:T(256)S(1)}, u32[]{:S(2)}) copy-start(f32[256]{0:T(256)S(1)} %get-tuple-element.436) | copy-start | bytes 3076
  266.8 146.3 %all-gather.17.cloned.1.call-start = ((), (), s32[]{:S(2)}) async-start(), calls=%async_computation.14 | async-start | bytes 1966080 | tf_op jit(solution)/shard_map/all_gather | solution.py:227
  267.5 532.0 %copy-start.73 = (f32[768]{0:T(1024)}, f32[768]{0:T(1024)S(1)}, u32[]{:S(2)}) copy-start(f32[768]{0:T(1024)S(1)} %get-tuple-element.434) | copy-start | bytes 9220
  299.6 40.7 %copy-start.8 = (bf16[256,768]{1,0:T(8,128)(2,1)S(1)}, bf16[256,768]{1,0:T(8,128)(2,1)}, u32[]{:S(2)}) copy-start(bf16[256,768]{1,0:T(8,128)(2,1)} %reduce-scatter.13.cloned.1.call-done) | copy-start | bytes 1179652
  338.2 461.3 %copy-start.83 = (f32[256]{0:T(256)}, f32[256]{0:T(256)S(1)}, u32[]{:S(2)}) copy-start(f32[256]{0:T(256)S(1)} %get-tuple-element.432) | copy-start | bytes 3076
  338.2 461.3 %copy-start.85 = (f32[256]{0:T(256)}, f32[256]{0:T(256)S(1)}, u32[]{:S(2)}) copy-start(f32[256]{0:T(256)S(1)} %get-tuple-element.433) | copy-start | bytes 3076
  340.3 46.2 %copy-start.91 = (f32[256]{0:T(256)}, f32[256]{0:T(256)S(1)}, u32[]{:S(2)}) copy-start(f32[256]{0:T(256)S(1)} %add_rsqrt_fusion.7) | copy-start | bytes 3076
  342.1 108.0 %reduce-scatter.23.cloned.1.call-start = ((), (), s32[]{:S(2)}) async-start(), calls=%async_computation.22 | async-start | bytes 1966080 | tf_op jit(solution)/shard_map/reduce_scatter | solution.py:245
  386.6 100.5 %reduce-scatter.15.cloned.1.call-start = ((), (), s32[]{:S(2)}) async-start(), calls=%async_computation.15 | async-start | bytes 1966080 | tf_op jit(solution)/shard_map/reduce_scatter | solution.py:237
  442.5 44.6 %copy-start.6 = (bf16[256,768]{1,0:T(8,128)(2,1)S(1)}, bf16[256,768]{1,0:T(8,128)(2,1)}, u32[]{:S(2)}) copy-start(bf16[256,768]{1,0:T(8,128)(2,1)} %reduce-scatter.17.cloned.1.call-done) | copy-start | bytes 1179652
  442.5 82.8 %all-gather.29.cloned.1.call-start = ((), (), s32[]{:S(2)}) async-start(), calls=%async_computation.28 | async-start | bytes 1966080 | tf_op jit(solution)/shard_map/all_gather | solution.py:227
  453.3 110.0 %all-gather.21.cloned.1.call-start = ((), (), s32[]{:S(2)}) async-start(), calls=%async_computation.18 | async-start | bytes 1966080 | tf_op jit(solution)/shard_map/all_gather | solution.py:227
  490.9 109.4 %reduce-scatter.31.cloned.1.call-start = ((), (), s32[]{:S(2)}) async-start(), calls=%async_computation.29 | async-start | bytes 1966080 | tf_op jit(solution)/shard_map/reduce_scatter | solution.py:245
  536.8 100.4 %reduce-scatter.19.cloned.1.call-start = ((), (), s32[]{:S(2)}) async-start(), calls=%async_computation.19 | async-start | bytes 1966080 | tf_op jit(solution)/shard_map/reduce_scatter | solution.py:237
  594.1 86.4 %all-gather.25.cloned.1.call-start = ((), (), s32[]{:S(2)}) async-start(), calls=%async_computation.23 | async-start | bytes 1966080 | tf_op jit(solution)/shard_map/all_gather | solution.py:259
  601.6 37.4 %copy-start.97 = (f32[256]{0:T(256)S(1)}, f32[256]{0:T(256)}, u32[]{:S(2)}) copy-start(f32[256]{0:T(256)} %copy-done.96) | copy-start | bytes 3076
  644.3 74.2 %all-gather.31.cloned.1.call-start = ((), (), s32[]{:S(2)}) async-start(), calls=%async_computation.30 | async-start | bytes 1966080 | tf_op jit(solution)/shard_map/all_gather | solution.py:259
  644.8 110.7 %reduce-scatter.25.cloned.1.call-start = ((), (), s32[]{:S(2)}) async-start(), calls=%async_computation.24 | async-start | bytes 1966080 | tf_op jit(solution)/shard_map/reduce_scatter | solution.py:265
  693.2 99.3 %reduce-scatter.33.cloned.1.call-start = ((), (), s32[]{:S(2)}) async-start(), calls=%async_computation.31 | async-start | bytes 1966080 | tf_op jit(solution)/shard_map/reduce_scatter | solution.py:265
  726.8 65.7 %copy-start.33 = (f32[256,768]{1,0:T(8,128)S(1)}, f32[256,768]{1,0:T(8,128)}, u32[]{:S(2)}) copy-start(f32[256,768]{1,0:T(8,128)} %get-tuple-element.411) | copy-start | bytes 2359300
  730.1 107.1 %all-gather.33.cloned.1.call-start = ((), (), s32[]{:S(2)}) async-start(), calls=%async_computation.32 | async-start | bytes 1966080 | tf_op jit(solution)/shard_map/all_gather | solution.py:275
  755.5 40.3 %copy-start.41 = (bf16[256,768]{1,0:T(8,128)(2,1)S(1)}, bf16[256,768]{1,0:T(8,128)(2,1)}, u32[]{:S(2)}) copy-start(bf16[256,768]{1,0:T(8,128)(2,1)} %reduce-scatter.25.cloned.1.call-done) | copy-start | bytes 1179652
  801.0 105.8 %all-gather.27.cloned.1.call-start = ((), (), s32[]{:S(2)}) async-start(), calls=%async_computation.25 | async-start | bytes 1966080 | tf_op jit(solution)/shard_map/all_gather | solution.py:275
  809.9 206.1 %reduce-scatter.35.cloned.1.call-start = ((), (), s32[]{:S(2)}) async-start(), calls=%async_computation.33 | async-start | bytes 1966080 | tf_op jit(solution)/shard_map/reduce_scatter | solution.py:286
  906.4 109.6 %reduce-scatter.27.cloned.1.call-start = ((), (), s32[]{:S(2)}) async-start(), calls=%async_computation.26 | async-start | bytes 1966080 | tf_op jit(solution)/shard_map/reduce_scatter | solution.py:286
  976.1 153.6 %all-reduce.4.cloned.1.call-start = ((), (), s32[]{:S(2)}) async-start(), calls=%async_computation.36 | async-start | bytes 14155776 | tf_op jit(solution)/shard_map/psum | solution.py:308
  1000.8 67.0 %copy-start.7 = (bf16[256,768]{1,0:T(8,128)(2,1)S(1)}, bf16[256,768]{1,0:T(8,128)(2,1)}, u32[]{:S(2)}) copy-start(bf16[256,768]{1,0:T(8,128)(2,1)} %reduce-scatter.17.cloned.1.call-done) | copy-start | bytes 1179652
  1000.8 67.0 %copy-start.14 = (f32[256,768]{1,0:T(8,128)S(1)}, f32[256,768]{1,0:T(8,128)}, u32[]{:S(2)}) copy-start(f32[256,768]{1,0:T(8,128)} %copy-done.13) | copy-start | bytes 2359300
  1000.8 67.0 %copy-start.84 = (f32[256]{0:T(256)S(1)}, f32[256]{0:T(256)}, u32[]{:S(2)}) copy-start(f32[256]{0:T(256)} %copy-done.83) | copy-start | bytes 3076
  1000.8 67.0 %copy-start.90 = (f32[256]{0:T(256)S(1)}, f32[256]{0:T(256)}, u32[]{:S(2)}) copy-start(f32[256]{0:T(256)} %add_rsqrt_fusion.5) | copy-start | bytes 3076
  1070.0 59.6 %copy-start.27 = (bf16[768,768]{1,0:T(8,128)(2,1)S(1)}, bf16[768,768]{1,0:T(8,128)(2,1)}, u32[]{:S(2)}) copy-start(bf16[768,768]{1,0:T(8,128)(2,1)} %param.33) | copy-start | bytes 3538948
  (105 other events, 815.7 us)
Sparse Core Ops, SparseCore 0:
  10.2 40.0 all-gather.34
  52.4 35.9 all-gather.36
  90.6 35.9 all-gather.18
  128.6 35.9 all-gather.14
  191.2 34.1 reduce-scatter.20
  228.1 34.2 reduce-scatter.28
  265.3 34.2 reduce-scatter.12
  302.5 34.2 reduce-scatter.16
  338.9 36.0 all-gather.22
  377.0 35.9 all-gather.16
  415.9 34.1 reduce-scatter.22
  452.8 34.2 reduce-scatter.14
  489.2 36.0 all-gather.28
  527.3 35.9 all-gather.20
  566.0 34.1 reduce-scatter.30
  603.0 34.2 reduce-scatter.18
  644.4 36.0 all-gather.24
  682.5 35.9 all-gather.30
  721.3 34.1 reduce-scatter.24
  758.2 34.2 reduce-scatter.32
  801.2 36.0 all-gather.32
  839.4 36.0 all-gather.26
  906.5 34.3 reduce-scatter.34
  976.2 34.5 reduce-scatter.26
  1015.4 114.2 all-reduce.3
where the time goes:
time: 1160 us; the launch traced here: 1150 us
  waiting for transfers between devices  618 us (53%)
  matrix products  290 us (25%)
  other arithmetic  99.2 us (9%)
  local copies, waits for them, and re-layouts  63.5 us (5%)
  blocking collectives  54.6 us (5%)
  between operations  19.7 us (2%)
    all_gather x4, waiting for transfers between devices, on_device(): lax.all_gather((first_quant, t_first.astype(jnp.bfloat16)), 'head', axis=...  120 us
    all_gather x4, waiting for transfers between devices, on_device(): lax.all_gather((x_quant, t_vals), 'head', axis=0, tiled=True)  108 us
    reduce_scatter x2, waiting for transfers between devices, on_device(): lax.psum_scatter(jnp.dot(ctx_quant, out_bin, preferred_element_type=jnp.f...  69.3 us
    reduce_scatter x2, waiting for transfers between devices, on_device(): lax.psum_scatter(jnp.dot(hidden_quant, ffn_out_bin, preferred_element_typ...  66.7 us
    reduce_scatter x2, waiting for transfers between devices, on_device(): lax.psum_scatter(matmul_nt(grad_hidden, ffn_in_bin).astype(jnp.bfloat16),...  62.3 us
    all_gather x2, waiting for transfers between devices, on_device(): lax.all_gather(grad_pre2.astype(jnp.bfloat16), 'head', axis=0, tiled=True)  60.8 us
    psum x1, waiting for transfers between devices, on_device(): direct_acc = list(lax.psum(to_latent(grad_bins), 'dp'))  58.4 us
    dot_general x2, matrix products, on_device(): jnp.dot(project_student_rows, ffn_in_bin, preferred_element_type=jnp.floa...  47.5 us
  transfers between devices with their start and end apart: 25, of which 22 were waited for; matrix products, arithmetic and copies ran while one was open for 34% of the time, Pallas kernels for 0%

commit v1 on v0

v1 whole, which is shorter than its diff:
```python
import functools

import jax
import jax.numpy as jnp
from jax import lax
from jax.experimental import pallas as pl
from jax.experimental.pallas import tpu as pltpu
from jax.sharding import PartitionSpec as P

D = 768
HD = 64
FF = 3072
SEQ = 512
MICRO = 2
GROUP = 8
PIECE = D // GROUP
HALF_PIECE = PIECE // 2
UNIT = 3 * HALF_PIECE
BIT_C, BIT_X, BIT_Y = 1, 2, 4
NEG = -1000000000.0
BF = jnp.bfloat16
F32 = jnp.float32
VMEM_LIMIT = 56 * 1024 * 1024

GATHERED = (
    ("first", (0, BIT_X)),
    ("first", (BIT_Y, BIT_Y | BIT_X)),
    ("first", (BIT_C, BIT_C | BIT_X)),
    ("first", (BIT_C | BIT_Y, BIT_C | BIT_Y | BIT_X)),
    ("second", (0, BIT_Y)),
    ("second", (BIT_X, BIT_X | BIT_Y)),
    ("second", (BIT_C, BIT_C | BIT_Y)),
    ("second", (BIT_C | BIT_X, BIT_C | BIT_X | BIT_Y)),
)


def nn(a, b):
    return lax.dot_general(a, b, (((1,), (0,)), ((), ())), preferred_element_type=F32)


def nt(a, b):
    return lax.dot_general(a, b, (((1,), (1,)), ((), ())), preferred_element_type=F32)


def tn(a, b):
    return lax.dot_general(a, b, (((0,), (0,)), ((), ())), preferred_element_type=F32)


def normalize(values):
    centred = values - jnp.mean(values, axis=-1, keepdims=True)
    inv_std = lax.rsqrt(jnp.mean(centred * centred, axis=-1, keepdims=True) + 1e-06)
    return centred * inv_std, inv_std


def norm_back(upstream, normed, inv_std, gain_vec):
    scaled = upstream * gain_vec
    centred_grad = (
        scaled
        - jnp.mean(scaled, axis=-1, keepdims=True)
        - normed * jnp.mean(scaled * normed, axis=-1, keepdims=True)
    )
    return centred_grad * inv_std


def colsum(values):
    return jnp.sum(values, axis=0, keepdims=True)


def start_weights(place, own, parts, full, sems):
    copies = []

    def go(src, dst):
        copy = pltpu.make_async_copy(src, dst, sems.at[len(copies)])
        copy.start()
        copies.append(copy)

    go(own, full.at[0])
    for (kind, flips), part in zip(GATHERED, parts):
        for unit, flip in enumerate(flips):
            row = pl.multiple_of((place ^ flip) * PIECE, PIECE)
            mid = pl.multiple_of(row + HALF_PIECE, HALF_PIECE)
            base = unit * UNIT
            if kind == "first":
                go(part.at[pl.ds(base, PIECE)], full.at[1, pl.ds(row, PIECE)])
                go(part.at[pl.ds(base + PIECE, HALF_PIECE)], full.at[2, pl.ds(row, HALF_PIECE)])
            else:
                go(part.at[pl.ds(base, HALF_PIECE)], full.at[2, pl.ds(mid, HALF_PIECE)])
                go(part.at[pl.ds(base + HALF_PIECE, PIECE)], full.at[3, pl.ds(row, PIECE)])
    return copies


N_COPIES = 1 + 4 * len(GATHERED)


def store_pieces(place, acc, keep_ref, send_ref, slot):
    for flip in range(GROUP):
        row = pl.multiple_of((place ^ flip) * PIECE, PIECE)
        target = send_ref if flip & 1 else keep_ref
        target[flip // 2, slot] = acc[pl.ds(row, PIECE), :].astype(BF)


def attend_forward(student, place_ref, clips_ref, *refs):
    xa, xb, seg_row, seg_col, gain, bias, own = refs[:7]
    parts = refs[7:15]
    if student:
        full, qkv_out, lse_out, ctx_out, pre_out, quant_out, quant_t_out, xq_out, xqt_out = refs[15:24]
        rows, mask_bias, attn, ctx_t, sems = refs[24:]
    else:
        qkv_out, first_out, first_low_out = refs[15:18]
        full, rows, mask_bias, attn, ctx_t, sems = refs[18:]
        xq_out = rows
    place = place_ref[0]
    copies = start_weights(place, own, parts, full, sems)
    half = xa.shape[0]
    slots = full.shape[0]
    heads = D // slots // HD
    width = heads * HD
    rows[:half, :] = xa[...]
    rows[half:, :] = xb[...]
    if student:
        level = clips_ref[0]
        xq = (level * jnp.tanh(rows[...].astype(F32) / level)).astype(BF)
        xq_out[...] = xq
        xqt_out[...] = xq.T
    mask_bias[...] = jnp.where(seg_col[...] == seg_row[...], 0.0, NEG)
    attn[...] = jnp.zeros_like(attn)
    for copy in copies:
        copy.wait()

    def slot_step(slot, carry):
        qkv = nn(xq_out[...], full[slot, :, : 3 * width]).astype(BF)
        qkv_out[slot] = qkv
        for head in range(heads):
            lo = head * HD
            queries = qkv[:, lo : lo + HD] * BF(0.125)
            key_rows = qkv[:, width + lo : width + lo + HD]
            value_rows = qkv[:, 2 * width + lo : 2 * width + lo + HD]
            scores = nt(key_rows, queries) + mask_bias[...]
            peak = jnp.max(scores, axis=0, keepdims=True)
            powers = jnp.exp(scores - peak)
            total = jnp.sum(powers, axis=0, keepdims=True)
            probs = (powers * (1.0 / total)).astype(BF)
            ctx_t[lo : lo + HD, :] = tn(value_rows, probs)
            if student:
                lse_out[slot, head : head + 1, :] = peak + jnp.log(total)
        context = ctx_t[...].T
        if student:
            ctx_out[slot] = context
            level = clips_ref[1]
            low = (level * jnp.tanh(context / level)).astype(BF)
        else:
            low = context.astype(BF)
        attn[...] += nt(low, full[slot, :, 3 * width :])
        return carry

    lax.fori_loop(0, slots, slot_step, 0)
    pre = rows[...].astype(F32) + attn[...]
    first = normalize(pre)[0] * gain[...] + bias[...]
    if student:
        pre_out[...] = pre
        level = clips_ref[2]
        quant = (level * jnp.tanh(first / level)).astype(BF)
        quant_out[...] = quant
        quant_t_out[...] = quant.T
    else:
        first_out[...] = first
        first_low_out[...] = first.astype(BF)


def hidden_forward(student, place_ref, clips_ref, *refs):
    quant, own = refs[:2]
    parts = refs[2:10]
    if student:
        full, act_out, act_t_out, slope_out, clip_out = refs[10:15]
        pre, sems = refs[15:]
    else:
        (act_out,) = refs[10:11]
        full, pre, sems = refs[11:]
    copies = start_weights(place_ref[0], own, parts, full, sems)
    for copy in copies:
        copy.wait()
    slots = full.shape[0]
    step = 64

    def slot_step(slot, carry):
        pre[...] = nn(quant[...], full[slot])

        def row_step(index, carry):
            at = pl.ds(pl.multiple_of(index * step, step), step)
            values = pre[at, :]
            cdf = 0.5 * (1.0 + lax.erf(values * 0.7071067811865476))
            act = values * cdf
            if student:
                level = clips_ref[3]
                inverse = 1.0 / level
                ratio = act * inverse
                tangent = jnp.tanh(ratio)
                act_out[slot, at, :] = (level * tangent).astype(BF)
                slope = 1.0 - tangent * tangent
                density = jnp.exp(-0.5 * values * values) * 0.3989422804014327
                slope_out[slot, at, :] = (slope * (cdf + values * density)).astype(BF)
                clip_out[slot, at, :] = (tangent - ratio * slope).astype(BF)
            else:
                act_out[slot, at, :] = act.astype(BF)
            return carry

        lax.fori_loop(0, SEQ // step, row_step, 0)
        if student:
            act_t_out[slot] = act_out[slot].T
        return carry

    lax.fori_loop(0, slots, slot_step, 0)


def output_forward(student, place_ref, *refs):
    act, gain, bias, own = refs[:4]
    parts = refs[4:12]
    if student:
        pre, gain_one, bias_one, t_result, grad_a, grad_b = refs[12:18]
        full, own_out, partner_out, grad_out, low_out, gain_out, bias_out = refs[18:25]
        acc, sems = refs[25:]
    else:
        (first_in,) = refs[12:13]
        (result_out,) = refs[13:14]
        full, acc, sems = refs[14:]
    copies = start_weights(place_ref[0], own, parts, full, sems)
    if student:
        acc[...] = normalize(pre[...])[0] * gain_one[...] + bias_one[...]
    else:
        acc[...] = first_in[...]
    for copy in copies:
        copy.wait()
    for slot in range(full.shape[0]):
        acc[...] += nn(act[slot], full[slot])
    normed, inv_std = normalize(acc[...])
    result = normed * gain[...] + bias[...]
    if not student:
        result_out[...] = result
        return
    half = grad_a.shape[0]
    own_out[...] = result[:half].astype(BF)
    partner_out[...] = result[half:].astype(BF)
    cotangent = jnp.concatenate([grad_a[...].astype(F32), grad_b[...].astype(F32)], axis=0)
    grad_result = cotangent + result - t_result[...]
    gain_out[...] = colsum(grad_result * normed)
    bias_out[...] = colsum(grad_result)
    grad_pre = norm_back(grad_result, normed, inv_std, gain[...])
    grad_out[...] = grad_pre
    low_out[...] = grad_pre.astype(BF)


def weight_grad(place_ref, left_t, right, keep_ref, send_ref, acc):
    def slot_step(slot, carry):
        left = left_t[slot] if len(left_t.shape) == 3 else left_t[...]
        rows = right[slot] if len(right.shape) == 3 else right[...]
        acc[...] = nn(left, rows)
        store_pieces(place_ref[0], acc, keep_ref, send_ref, slot)
        return carry

    lax.fori_loop(0, keep_ref.shape[1], slot_step, 0)


def hidden_back(grad_low, full, slope, clip, grad_out, clip_out):
    clip_out[...] = jnp.zeros_like(clip_out)

    def slot_step(slot, carry):
        grad = nt(grad_low[...], full[slot])
        grad_out[slot] = (grad * slope[slot].astype(F32)).astype(BF)
        clip_out[...] += colsum(grad * clip[slot].astype(F32))
        return carry

    lax.fori_loop(0, full.shape[0], slot_step, 0)


def first_back(
    clips_ref, grad_hidden, full, pre, gain, bias, grad_two,
    grad_out, low_out, low_t_out, gain_out, bias_out, clip_out, acc,
):
    acc[...] = jnp.zeros_like(acc)

    def slot_step(slot, carry):
        acc[...] += nt(grad_hidden[slot], full[slot])
        return carry

    lax.fori_loop(0, full.shape[0], slot_step, 0)
    normed, inv_std = normalize(pre[...])
    first = normed * gain[...] + bias[...]
    level = clips_ref[2]
    ratio = first / level
    tangent = jnp.tanh(ratio)
    slope = 1.0 - tangent * tangent
    grad_fq = acc[...]
    clip_out[...] = colsum(grad_fq * (tangent - ratio * slope))
    upstream = grad_fq * slope + grad_two[...]
    gain_out[...] = colsum(upstream * normed)
    bias_out[...] = colsum(upstream)
    grad_pre = norm_back(upstream, normed, inv_std, gain[...])
    grad_out[...] = grad_pre
    low = grad_pre.astype(BF)
    low_out[...] = low
    low_t_out[...] = low.T


def attend_back(first, last, place_ref, clips_ref, *refs):
    seg_row, seg_col, qkv, t_qkv, lse, ctx, low, low_t, xq_t, full = refs[:10]
    rest = list(refs[10:])
    grad_in = None if first else rest.pop(0)
    if last:
        grad_one, xa, xb = rest[:3]
        rest = rest[3:]
    keep_ref, send_ref, clip_one_out = rest[:3]
    rest = rest[3:]
    if last:
        own_out, partner_out, clip_zero_out = rest[:3]
        rest = rest[3:]
    else:
        grad_out = rest.pop(0)
    mask_bias, mask_scale, grad_qkv, acc = rest
    same = seg_col[...] == seg_row[...]
    mask_bias[...] = jnp.where(same, 0.0, NEG)
    mask_scale[...] = jnp.where(same, 1.0 / SEQ, 0.0)
    width = ctx.shape[-1]
    heads = width // HD
    level = clips_ref[1]
    context = ctx[0]
    ratio = context / level
    tangent = jnp.tanh(ratio)
    slope = 1.0 - tangent * tangent
    grad_cq = nn(low[...], full[0, :, 3 * width :])
    clip_one_out[...] = colsum(grad_cq * (tangent - ratio * slope))
    grad_ctx = (grad_cq * slope).astype(BF)
    acc[:, 3 * width :] = nn(low_t[...], (level * tangent).astype(BF))
    for head in range(heads):
        lo = head * HD
        queries = qkv[0, :, lo : lo + HD] * BF(0.125)
        key_rows = qkv[0, :, width + lo : width + lo + HD]
        value_rows = qkv[0, :, 2 * width + lo : 2 * width + lo + HD]
        t_queries = t_qkv[0, :, lo : lo + HD] * BF(0.125)
        t_keys = t_qkv[0, :, width + lo : width + lo + HD]
        upstream = grad_ctx[:, lo : lo + HD]
        scores = nt(key_rows, queries)
        probs = jnp.exp(scores + mask_bias[...] - lse[0, head : head + 1, :])
        grad_probs = nt(value_rows, upstream)
        grad_values = nn(probs.astype(BF), upstream)
        row_sum = jnp.sum(probs * grad_probs, axis=0, keepdims=True)
        gap = scores - nt(t_keys, t_queries)
        grad_scores = (probs * (grad_probs - row_sum) + gap * mask_scale[...]).astype(BF)
        grad_keys = nn(grad_scores, queries)
        grad_queries = tn(key_rows, grad_scores).T * 0.125
        grad_qkv[:, lo : lo + HD] = grad_queries.astype(BF)
        grad_qkv[:, width + lo : width + lo + HD] = grad_keys.astype(BF)
        grad_qkv[:, 2 * width + lo : 2 * width + lo + HD] = grad_values.astype(BF)
    acc[:, : 3 * width] = nn(xq_t[...], grad_qkv[...])
    store_pieces(place_ref[0], acc, keep_ref, send_ref, 0)
    grad_xq = nt(grad_qkv[...], full[0, :, : 3 * width])
    if not first:
        grad_xq = grad_xq + grad_in[...]
    if not last:
        grad_out[...] = grad_xq
        return
    half = xa.shape[0]
    level = clips_ref[0]
    total = jnp.zeros((1, D), F32)
    for start, x_ref, out in ((0, xa, own_out), (half, xb, partner_out)):
        ratio = x_ref[...].astype(F32) / level
        tangent = jnp.tanh(ratio)
        slope = 1.0 - tangent * tangent
        grad = grad_xq[start : start + half]
        total = total + colsum(grad * (tangent - ratio * slope))
        out[...] = (grad * slope + grad_one[start : start + half, :]).astype(out.dtype)
    clip_zero_out[...] = total


def finish(place_ref, own_piece, p1, p2, p3, p4, p5, latent, scale, out):
    place = place_ref[0]

    def put(flip, first_half, source, unit):
        row = (place ^ flip) * PIECE + (0 if first_half else HALF_PIECE)
        at = pl.ds(pl.multiple_of(row, HALF_PIECE), HALF_PIECE)
        values = source[unit * HALF_PIECE : (unit + 1) * HALF_PIECE, :].astype(F32)
        out[at, :] = values + scale[...] * latent[at, :].astype(F32)

    put(0, True, own_piece, 0)
    put(0, False, own_piece, 1)
    put(BIT_X, True, p1, 0)
    put(BIT_Y, False, p1, 1)
    put(BIT_Y, True, p2, 0)
    put(BIT_Y | BIT_X, True, p2, 1)
    put(BIT_X, False, p3, 0)
    put(BIT_X | BIT_Y, False, p3, 1)
    for unit, flip in enumerate((0, BIT_X, BIT_Y, BIT_Y | BIT_X)):
        put(BIT_C | flip, True, p4, unit)
    for unit, flip in enumerate((0, BIT_Y, BIT_X, BIT_X | BIT_Y)):
        put(BIT_C | flip, False, p5, unit)


VM = pl.BlockSpec(memory_space=pltpu.VMEM)
SM = pl.BlockSpec(memory_space=pltpu.SMEM)
ANY = pl.BlockSpec(memory_space=pl.ANY)
DMA_SEMS = pltpu.SemaphoreType.DMA((N_COPIES,))


def shape(dims, dtype):
    return jax.ShapeDtypeStruct(dims, dtype)


def call(name, body, args, specs, outs, scratch, flops, out_specs=None, grid=None):
    total = sum(a.size * a.dtype.itemsize for a in args) + sum(
        o.size * o.dtype.itemsize for o in outs
    )
    return pl.pallas_call(
        body,
        name=name,
        grid=grid or (),
        in_specs=specs,
        out_specs=out_specs or [VM] * len(outs),
        out_shape=outs,
        scratch_shapes=scratch,
        compiler_params=pltpu.CompilerParams(vmem_limit_bytes=VMEM_LIMIT),
        cost_estimate=pl.CostEstimate(flops=flops, bytes_accessed=total, transcendentals=0),
    )(*args)


def flip_pairs(size, bit):
    return [(i, i ^ bit) for i in range(size)]


def swap(array, axis, size, bit):
    return lax.ppermute(array, axis, flip_pairs(size, bit))


def ring(array, size, step):
    return lax.ppermute(array, "head", [(i, (i + step) % size) for i in range(size)])


def gather_pieces(piece, dp, n):
    z = [ring(piece, n, step) for step in range(1, n)]
    first = jnp.concatenate([z[0], z[1][:HALF_PIECE]])
    second = jnp.concatenate([z[1][HALF_PIECE:], z[2]])
    first = jnp.concatenate([first, swap(first, "dp", dp, BIT_X)])
    second = jnp.concatenate([second, swap(second, "dp", dp, BIT_Y)])
    first_far = swap(first, "dp", dp, BIT_Y)
    second_far = swap(second, "dp", dp, BIT_X)
    return (
        first,
        first_far,
        swap(first, "dp", dp, BIT_C),
        swap(first_far, "dp", dp, BIT_C),
        second,
        second_far,
        swap(second, "dp", dp, BIT_C),
        swap(second_far, "dp", dp, BIT_C),
    )


def reduce_pieces(keep, send, dp):
    got = swap(send, "dp", dp, BIT_C)
    total = keep.astype(F32) + got.astype(F32)
    top, low = total[:, :, :HALF_PIECE], total[:, :, HALF_PIECE:]
    top_got = swap(jnp.stack([top[1], top[3]]).astype(BF), "dp", dp, BIT_X).astype(F32)
    low_got = swap(jnp.stack([low[2], low[3]]).astype(BF), "dp", dp, BIT_Y).astype(F32)
    top_two = swap((top[2] + top_got[1]).astype(BF), "dp", dp, BIT_Y).astype(F32)
    low_two = swap((low[1] + low_got[1]).astype(BF), "dp", dp, BIT_X).astype(F32)
    mine = jnp.concatenate(
        [top[0] + top_got[0] + top_two, low[0] + low_got[0] + low_two], axis=1
    )
    bit = GROUP
    while bit < dp:
        mine = mine + swap(mine.astype(BF), "dp", dp, bit).astype(F32)
        bit *= 2
    return mine


def reduce_slots(pieces, n):
    total = pieces[0]
    for step in range(1, n):
        total = total + ring(pieces[step].astype(BF), n, -step).astype(F32)
    return total


def share_pieces(piece, dp):
    top, low = piece[:HALF_PIECE], piece[HALF_PIECE:]
    top_x = swap(top, "dp", dp, BIT_X)
    low_y = swap(low, "dp", dp, BIT_Y)
    pair = jnp.concatenate([top, top_x])
    pair_low = jnp.concatenate([low, low_y])
    near = jnp.concatenate([top_x, low_y])
    far = swap(pair, "dp", dp, BIT_Y)
    far_low = swap(pair_low, "dp", dp, BIT_X)
    other = swap(jnp.concatenate([pair, far]), "dp", dp, BIT_C)
    other_low = swap(jnp.concatenate([pair_low, far_low]), "dp", dp, BIT_C)
    return near, far, far_low, other, other_low


def sum_over(values, sizes):
    for axis, size in sizes:
        bit = 1
        while bit < size:
            values = values + swap(values, axis, size, bit)
            bit *= 2
    return values


def on_device(
    dp,
    n,
    hidden_in,
    teacher_in,
    out_grad,
    segment_ids,
    qkv_latent,
    out_latent,
    ffn_in_latent,
    ffn_out_latent,
    norm_gain,
    norm_bias,
    clips,
    teacher_qkv,
    teacher_out,
    teacher_ffn_in,
    teacher_ffn_out,
    teacher_gain,
    teacher_bias,
):
    h = lax.axis_index("head")
    place = lax.axis_index("dp") % GROUP
    parity = h % MICRO
    half = hidden_in.shape[1]
    width = qkv_latent.shape[-1]
    heads = width // HD
    place_arr = place.astype(jnp.int32).reshape(1)

    def pick(array, index):
        return lax.dynamic_index_in_dim(array, index, 0, keepdims=False)

    def exchange(array):
        return swap(array, "head", n, 1)

    def piece_of(array):
        return lax.dynamic_slice_in_dim(array, place * PIECE, PIECE, axis=0)

    x_own = pick(hidden_in, parity)
    x_far = exchange(pick(hidden_in, 1 - parity))
    t_own = pick(teacher_in, parity)
    t_far = exchange(pick(teacher_in, 1 - parity))
    g_own = pick(out_grad, parity)
    g_far = exchange(pick(out_grad, 1 - parity))
    seg = pick(pick(segment_ids, parity), h // MICRO)
    seg = jnp.where(parity == 0, seg, jnp.concatenate([seg[half:], seg[:half]]))
    seg_row, seg_col = seg.reshape(1, SEQ), seg.reshape(SEQ, 1)

    def attention_weights(qkv, out):
        return jnp.concatenate([qkv[0], qkv[1], qkv[2], out.T], axis=1)

    t_attn = attention_weights(teacher_qkv, teacher_out)
    t_attn_parts = gather_pieces(piece_of(t_attn), dp, n)

    latents = [attention_weights(qkv_latent, out_latent), ffn_in_latent, ffn_out_latent]
    columns = jnp.sum(jnp.square(latents[0].astype(F32)), axis=0).reshape(4, width).sum(axis=1)
    squares = jnp.concatenate(
        [
            columns,
            jnp.sum(jnp.square(ffn_in_latent.astype(F32))).reshape(1),
            jnp.sum(jnp.square(ffn_out_latent.astype(F32))).reshape(1),
        ]
    )
    totals = sum_over(jnp.pad(squares, (0, 122)).reshape(1, 128), [("head", n)])[0, :6]
    entries = jnp.array([D * D, D * D, D * D, D * D, D * FF, FF * D], F32)
    levels_six = jnp.sqrt(totals / entries + 1e-06)
    levels = [
        jnp.repeat(levels_six[:4], width, total_repeat_length=D).reshape(1, D),
        levels_six[4].reshape(1, 1),
        levels_six[5].reshape(1, 1),
    ]

    def binarize(latent, level):
        return (level * jnp.tanh(2.0 * latent.astype(F32) / level)).astype(BF)

    bins = [binarize(latent, level) for latent, level in zip(latents, levels)]
    s_parts = [None] * 3
    s_parts[0] = gather_pieces(piece_of(bins[0]), dp, n)
    t_in_parts = gather_pieces(piece_of(teacher_ffn_in), dp, n)
    s_parts[1] = gather_pieces(piece_of(bins[1]), dp, n)
    t_out_parts = gather_pieces(piece_of(teacher_ffn_out), dp, n)
    s_parts[2] = gather_pieces(piece_of(bins[2]), dp, n)

    row = lambda array, index: array[index].reshape(1, D)
    big = pltpu.VMEM((n, D, D), BF)
    mm = 2 * SEQ * D * D

    attn_scratch = [
        pltpu.VMEM((SEQ, D), BF),
        pltpu.VMEM((SEQ, SEQ), F32),
        pltpu.VMEM((SEQ, D), F32),
        pltpu.VMEM((width, SEQ), F32),
        DMA_SEMS,
    ]
    t_qkv, t_first, t_first_low = call(
        "teacher_attend",
        functools.partial(attend_forward, False),
        (place_arr, clips, t_own, t_far, seg_row, seg_col, row(teacher_gain, 0), row(teacher_bias, 0), t_attn)
        + t_attn_parts,
        [SM, SM] + [VM] * 6 + [ANY] * 9,
        [shape((n, SEQ, 3 * width), BF), shape((SEQ, D), F32), shape((SEQ, D), BF)],
        [big] + attn_scratch,
        8 * mm,
    )
    full_attn, qkv, lse, ctx, pre_one, quant, quant_t, xq, xq_t = call(
        "student_attend",
        functools.partial(attend_forward, True),
        (place_arr, clips, x_own, x_far, seg_row, seg_col, row(norm_gain, 0), row(norm_bias, 0), bins[0])
        + s_parts[0],
        [SM, SM] + [VM] * 6 + [ANY] * 9,
        [
            shape((n, D, D), BF),
            shape((n, SEQ, 3 * width), BF),
            shape((n, 8, SEQ), F32),
            shape((n, SEQ, width), F32),
            shape((SEQ, D), F32),
            shape((SEQ, D), BF),
            shape((D, SEQ), BF),
            shape((SEQ, D), BF),
            shape((D, SEQ), BF),
        ],
        attn_scratch,
        8 * mm,
    )
    (t_act,) = call(
        "teacher_hidden",
        functools.partial(hidden_forward, False),
        (place_arr, clips, t_first_low, teacher_ffn_in) + t_in_parts,
        [SM, SM, VM] + [ANY] * 9,
        [shape((n, SEQ, D), BF)],
        [big, pltpu.VMEM((SEQ, D), F32), DMA_SEMS],
        6 * mm,
    )
    full_in, act, act_t, slope, clip_term = call(
        "student_hidden",
        functools.partial(hidden_forward, True),
        (place_arr, clips, quant, bins[1]) + s_parts[1],
        [SM, SM, VM] + [ANY] * 9,
        [
            shape((n, D, D), BF),
            shape((n, SEQ, D), BF),
            shape((n, D, SEQ), BF),
            shape((n, SEQ, D), BF),
            shape((n, SEQ, D), BF),
        ],
        [pltpu.VMEM((SEQ, D), F32), DMA_SEMS],
        8 * mm,
    )
    (t_result,) = call(
        "teacher_output",
        functools.partial(output_forward, False),
        (place_arr, t_act, row(teacher_gain, 1), row(teacher_bias, 1), teacher_ffn_out) + t_out_parts + (t_first,),
        [SM] + [VM] * 3 + [ANY] * 9 + [VM],
        [shape((SEQ, D), F32)],
        [big, pltpu.VMEM((SEQ, D), F32), DMA_SEMS],
        4 * mm,
    )
    full_out, out_own, out_far, grad_two, low_two, gain_two, bias_two = call(
        "student_output",
        functools.partial(output_forward, True),
        (place_arr, act, row(norm_gain, 1), row(norm_bias, 1), bins[2])
        + s_parts[2]
        + (pre_one, row(norm_gain, 0), row(norm_bias, 0), t_result, g_own, g_far),
        [SM] + [VM] * 3 + [ANY] * 9 + [VM] * 6,
        [
            shape((n, D, D), BF),
            shape((half, D), BF),
            shape((half, D), BF),
            shape((SEQ, D), F32),
            shape((SEQ, D), BF),
            shape((1, D), F32),
            shape((1, D), F32),
        ],
        [pltpu.VMEM((SEQ, D), F32), DMA_SEMS],
        4 * mm,
    )

    def grad_call(name, left_t, right):
        return call(
            name,
            weight_grad,
            (place_arr, left_t, right),
            [SM, VM, VM],
            [shape((GROUP // 2, n, PIECE, D), BF)] * 2,
            [pltpu.VMEM((D, D), F32)],
            4 * mm,
        )

    grad_out_w = reduce_pieces(*grad_call("ffn_out_weight", act_t, low_two), dp)
    grad_hidden, clip_three = call(
        "hidden_back",
        hidden_back,
        (low_two, full_out, slope, clip_term),
        [VM] * 4,
        [shape((n, SEQ, D), BF), shape((1, D), F32)],
        [],
        5 * mm,
    )
    grad_in_w = reduce_pieces(*grad_call("ffn_in_weight", quant_t, grad_hidden), dp)
    grad_one, low_one, low_one_t, gain_one, bias_one, clip_two = call(
        "first_back",
        first_back,
        (clips, grad_hidden, full_in, pre_one, row(norm_gain, 0), row(norm_bias, 0), grad_two),
        [SM] + [VM] * 6,
        [
            shape((SEQ, D), F32),
            shape((SEQ, D), BF),
            shape((D, SEQ), BF),
            shape((1, D), F32),
            shape((1, D), F32),
            shape((1, D), F32),
        ],
        [pltpu.VMEM((SEQ, D), F32)],
        4 * mm,
    )
    clip_one = jnp.zeros((1, width), F32)
    grad_xq = None
    attn_slots = []
    for slot in range(n):
        first, last = slot == 0, slot == n - 1

        def at(*dims, slot=slot):
            return pl.BlockSpec((1,) + dims, lambda i: (slot, 0, 0))

        def whole(*dims):
            return pl.BlockSpec(dims, lambda i: (0,) * len(dims))

        args = [place_arr, clips, seg_row, seg_col, qkv, t_qkv, lse, ctx, low_one, low_one_t, xq_t, full_attn]
        specs = [
            SM,
            SM,
            whole(1, SEQ),
            whole(SEQ, 1),
            at(SEQ, 3 * width),
            at(SEQ, 3 * width),
            at(8, SEQ),
            at(SEQ, width),
            whole(SEQ, D),
            whole(D, SEQ),
            whole(D, SEQ),
            at(D, D),
        ]
        if not first:
            args.append(grad_xq)
            specs.append(whole(SEQ, D))
        outs = [shape((GROUP // 2, 1, PIECE, D), BF)] * 2 + [shape((1, width), F32)]
        if last:
            args += [grad_one, x_own, x_far]
            specs += [whole(SEQ, D), whole(half, D), whole(half, D)]
            outs += [shape((half, D), F32), shape((half, D), BF), shape((1, D), F32)]
        else:
            outs += [shape((SEQ, D), F32)]
        results = pl.pallas_call(
            functools.partial(attend_back, first, last),
            name="attend_back",
            grid=(1,),
            in_specs=specs,
            out_specs=[whole(*o.shape) for o in outs],
            out_shape=outs,
            scratch_shapes=[
                pltpu.VMEM((SEQ, SEQ), F32),
                pltpu.VMEM((SEQ, SEQ), F32),
                pltpu.VMEM((SEQ, 3 * width), BF),
                pltpu.VMEM((D, D), F32),
            ],
            compiler_params=pltpu.CompilerParams(vmem_limit_bytes=VMEM_LIMIT),
            cost_estimate=pl.CostEstimate(flops=5 * mm, bytes_accessed=12 << 20, transcendentals=0),
        )(*args)
        attn_slots.append(reduce_pieces(results[0], results[1], dp)[0])
        clip_one = clip_one + results[2]
        if not last:
            grad_xq = results[3]
    in_grad_own, in_grad_far, clip_zero = results[3:6]

    everywhere = [("dp", dp), ("head", n)]
    norms = sum_over(jnp.concatenate([gain_one, gain_two, bias_one, bias_two]), everywhere)
    pieces = [
        reduce_slots(attn_slots, n),
        reduce_slots([grad_in_w[slot] for slot in range(n)], n),
        reduce_slots([grad_out_w[slot] for slot in range(n)], n),
    ]
    direct, scale_terms = [], []
    for piece, latent, level in zip(pieces, latents, levels):
        unit = 2.0 * piece_of(latent).astype(F32) / level
        tangent = jnp.tanh(unit)
        slope_sq = 1.0 - tangent * tangent
        direct.append((piece * 2.0 * slope_sq).astype(BF))
        scale_terms.append(jnp.sum(piece * (tangent - unit * slope_sq), axis=0))
    scalars = jnp.concatenate(
        [
            scale_terms[0].reshape(4, width).sum(axis=1),
            jnp.stack(
                [
                    jnp.sum(scale_terms[1]),
                    jnp.sum(scale_terms[2]),
                ]
            ),
            jnp.stack([jnp.sum(clip_zero), jnp.sum(clip_one), jnp.sum(clip_two), jnp.sum(clip_three)]),
        ]
    )
    repeats = dp // GROUP
    weights = jnp.array([1.0 / repeats] * 6 + [1.0] * 4, F32)
    sums = sum_over(jnp.pad(scalars * weights, (0, 118)).reshape(1, 128), everywhere)[0]
    scales = sums[:6] / (entries * levels_six)
    scale_rows = [
        jnp.repeat(scales[:4], width, total_repeat_length=D).reshape(1, D),
        jnp.broadcast_to(scales[4].reshape(1, 1), (1, D)),
        jnp.broadcast_to(scales[5].reshape(1, 1), (1, D)),
    ]
    finals = []
    for piece, latent, scale_row in zip(direct, latents, scale_rows):
        finals.append(
            call(
                "finish",
                finish,
                (place_arr, piece) + share_pieces(piece, dp) + (latent, scale_row),
                [SM] + [VM] * 8,
                [shape((D, D), F32)],
                [],
                0,
            )[0]
        )
    attn_grad = finals[0]
    qkv_grad = jnp.stack([attn_grad[:, j * width : (j + 1) * width] for j in range(3)])

    def both(own, far):
        first_row = jnp.where(parity == 0, own, far)
        second_row = jnp.where(parity == 0, far, own)
        return jnp.stack([first_row, second_row])

    return (
        both(out_own, exchange(out_far)),
        both(in_grad_own, exchange(in_grad_far).astype(F32)),
        qkv_grad,
        attn_grad[:, 3 * width :].T,
        finals[1],
        finals[2],
        norms[:2],
        norms[2:],
        sums[6:10],
    )


def solution(mesh):
    placed = (
        P(None, ("dp", "head"), None),
        P(None, ("dp", "head"), None),
        P(None, ("dp", "head"), None),
        P(None, "dp", None),
        P(None, None, "head"),
        P("head", None),
        P(None, "head"),
        P("head", None),
        P(),
        P(),
        P(),
        P(None, None, "head"),
        P("head", None),
        P(None, "head"),
        P("head", None),
        P(),
        P(),
    )
    return jax.shard_map(
        functools.partial(on_device, mesh.shape["dp"], mesh.shape["head"]),
        mesh=mesh,
        in_specs=placed,
        out_specs=(
            P(None, ("dp", "head"), None),
            P(None, ("dp", "head"), None),
            P(None, None, "head"),
            P("head", None),
            P(None, "head"),
            P("head", None),
            P(),
            P(),
            P(),
        ),
        check_vma=False,
    )
```

time: 1160 us -> 559 us (0.48)
  waiting for transfers between devices: 618 us -> 141 us
  matrix products: 290 us -> 0 us
  Pallas kernels: 0 us -> 170 us
  starting transfers between devices: 2.98 us -> 128 us
  blocking collectives: 54.6 us -> 0 us
  other arithmetic: 99.2 us -> 61.4 us
  local copies, waits for them, and re-layouts: 63.5 us -> 45 us
  between operations: 19.7 us -> 3.08 us
    all_gather x12 -> x0, waiting for transfers between devices: 316 us -> none  [the longest x4 120 us: on_device(): lax.all_gather((first_quant, t_first.astype(jnp.bfloat16)), 'head', axis=...]
    dot_general x62 -> x0, matrix products: 268 us -> none  [the longest x2 47.5 us: on_device(): jnp.dot(project_student_rows, ffn_in_bin, preferred_element_type=jnp.floa...]
    reduce_scatter x12 -> x0, waiting for transfers between devices: 241 us -> none  [the longest x2 69.3 us: on_device(): lax.psum_scatter(jnp.dot(ctx_quant, out_bin, preferred_element_type=jnp.f...]
    pallas_call x0 -> x17, Pallas kernels: none -> 170 us  [the longest x13 132 us: call(): pl.pallas_call(body, name=name, grid=grid or (), in_specs=specs, out_spec...]
    ppermute x0 -> x140, waiting for transfers between devices: none -> 141 us  [the longest x113 95 us: swap(): return lax.ppermute(array, axis, flip_pairs(size, bit))]
    ppermute x0 -> x140, starting transfers between devices: none -> 128 us  [the longest x113 91.2 us: swap(): return lax.ppermute(array, axis, flip_pairs(size, bit))]
    psum x1 -> x0, waiting for transfers between devices: 58.4 us -> none  [on_device(): direct_acc = list(lax.psum(to_latent(grad_bins), 'dp'))]
    psum x2 -> x0, blocking collectives: 54.6 us -> none  [the longest x1 40.8 us: on_device(): lax.psum((rms_local, gain_acc, bias_acc, clip_acc), ('dp', 'head'))]
  transfers between devices with their start and end apart: 25 -> 140, of which waited for: 22 -> 45; matrix products, arithmetic and copies ran while one was open for 34% -> 16% of each run, Pallas kernels for 0% -> 25%
where the time goes in v1:
time: 559 us; the launch traced here: 549 us
  Pallas kernels  170 us (30%)
  waiting for transfers between devices  141 us (25%)
  starting transfers between devices  128 us (23%)
  other arithmetic  61.4 us (11%)
  local copies, waits for them, and re-layouts  45 us (8%)
    pallas_call x13, Pallas kernels, call(): pl.pallas_call(body, name=name, grid=grid or (), in_specs=specs, out_spec...  132 us
    ppermute x113, waiting for transfers between devices, swap(): return lax.ppermute(array, axis, flip_pairs(size, bit))  95 us
    ppermute x113, starting transfers between devices, swap(): return lax.ppermute(array, axis, flip_pairs(size, bit))  91.2 us
    ppermute x27, waiting for transfers between devices, ring(): lax.ppermute(array, 'head', [(i, (i + step) % size) for i in range(size)])  46.1 us
    pallas_call x4, Pallas kernels, on_device(): pl.pallas_call(functools.partial(attend_back, first, last), name='attend_...  38.6 us
    ppermute x27, starting transfers between devices, ring(): lax.ppermute(array, 'head', [(i, (i + step) % size) for i in range(size)])  36.8 us
    unnamed x210, local copies, waits for them, and re-layouts  14.2 us
  transfers between devices with their start and end apart: 140, of which 45 were waited for; matrix products, arithmetic and copies ran while one was open for 16% of the time, Pallas kernels for 25%

profile of v1, /device:TPU:0, one launch (start us, length us, event | category | flops | bytes accessed | tf_op | source)
XLA Modules:
  0.0 549.0 jit_solution(2349445345914766614)
XLA Ops:
  2.4 5.0 collective-permute-start.65
  10.0 2.8 collective-permute-start.54
  50.5 2.6 select_select_fusion.1
  60.6 6.7 %collective-permute-done.38 = bf16[96,768]{1,0:T(8,128)(2,1)S(1)} collective-permute-done((bf16[96,768]{1,0:T(8,128)(2,1)S(1)}, bf16[96,768]{1,0:T(8,128)(2,1)S(1)}, u32[]{:S(2)}, u32[]{:S(2)}) %collective-permute-start.38) | collective-permute-done | bytes 147488 | tf_op jit(solution)/shard_map/ppermute | solution.py:433
  69.4 3.6 collective-permute-start.9
  81.3 7.9 %collective-permute-done.4 = bf16[96,768]{1,0:T(8,128)(2,1)S(1)} collective-permute-done((bf16[96,768]{1,0:T(8,128)(2,1)S(1)}, bf16[96,768]{1,0:T(8,128)(2,1)S(1)}, u32[]{:S(2)}, u32[]{:S(2)}) %collective-permute-start.4) | collective-permute-done | bytes 147488 | tf_op jit(solution)/shard_map/ppermute | solution.py:433
  89.2 10.5 %collective-permute-done.26 = bf16[96,768]{1,0:T(8,128)(2,1)S(1)} collective-permute-done((bf16[96,768]{1,0:T(8,128)(2,1)S(1)}, bf16[96,768]{1,0:T(8,128)(2,1)S(1)}, u32[]{:S(2)}, u32[]{:S(2)}) %collective-permute-start.26) | collective-permute-done | bytes 147488 | tf_op jit(solution)/shard_map/ppermute | solution.py:433
  106.9 5.1 collective-permute-done.15
  117.7 2.7 collective-permute-done.50
  127.2 2.7 collective-permute-done.5
  148.7 7.5 %collective-permute-done.56.refs_7_ = bf16[288,768]{1,0:T(8,128)(2,1)} collective-permute-done((bf16[288,768]{1,0:T(8,128)(2,1)S(1)}, bf16[288,768]{1,0:T(8,128)(2,1)}, u32[]{:S(2)}, u32[]{:S(2)}) %collective-permute-start.56) | collective-permute-done | bytes 442400 | tf_op jit(solution)/shard_map/ppermute | solution.py:429
  156.3 2.5 collective-permute-start.40
  161.2 4.5 collective-permute-done.67.refs_9_
  170.1 4.5 collective-permute-done.45.refs_12_
  180.6 16.9 %teacher_attend.1 = (bf16[4,512,576]{2,1,0:T(8,128)(2,1)}, f32[512,768]{1,0:T(8,128)}, bf16[512,768]{1,0:T(8,128)(2,1)}) custom-call(s32[1]{0:T(128)} %bitcast.place_ref, f32[4]{0:T(128)} %clips_ref.17, bf16[256,768]{1,0:T(8,128)(2,1)} %get-tuple-element.237.refs_0_, bf16[256,768]{1,0:T(8,128)(2,1)} %collective-permute-done.36.refs_1_, ...), custom_call_target="tpu_custom_call" | custom-call | flops 4831838208 | bytes 10233876 | tf_op jit(solution)/shard_map/teacher_attend/pallas_call | solution.py:411
  201.7 10.1 %teacher_hidden.1.refs_0_ = bf16[4,512,768]{2,1,0:T(8,128)(2,1)} custom-call(s32[1]{0:T(128)} %bitcast.place_ref, f32[4]{0:T(128)} %clips_ref.17, bf16[512,768]{1,0:T(8,128)(2,1)} %get-tuple-element.86.refs_0_, bf16[768,768]{1,0:T(8,128)(2,1)} %refs_1_.1, bf16[288,768]{1,0:T(8,128)(2,1)} %copy-done.34, bf16[288,768]{1,0:T(8,128)(2,1)} %collective-permute-done.51.refs_3_, ...), custom_call_target="tpu_custom_call" | custom-call | flops 3623878656 | bytes 8650772 | tf_op jit(solution)/shard_map/teacher_hidden/pallas_call | solution.py:411
  211.8 9.1 %teacher_output.1.refs_15_ = f32[512,768]{1,0:T(8,128)} custom-call(s32[1]{0:T(128)} %bitcast.place_ref, bf16[4,512,768]{2,1,0:T(8,128)(2,1)} %teacher_hidden.1.refs_0_, f32[1,768]{1,0:T(1,128)} %get-tuple-element.289.refs_1_, f32[1,768]{1,0:T(1,128)} %get-tuple-element.287.refs_2_, bf16[768,768]{1,0:T(8,128)(2,1)} %refs_3_.1, bf16[288,768]{1,0:T(8,128)(2,1)} %copy-done.10, ...), custom_call_target="tpu_custom_call" | custom-call | flops 2415919104 | bytes 11016196 | tf_op jit(solution)/shard_map/teacher_output/pallas_call | solution.py:411
  222.6 17.5 %student_attend.1 = (bf16[4,768,768]{2,1,0:T(8,128)(2,1)}, bf16[4,512,576]{2,1,0:T(8,128)(2,1)}, f32[4,8,512]{2,1,0:T(8,128)}, f32[4,512,192]{2,1,0:T(8,128)}, f...) custom-call(s32[1]{0:T(128)} %bitcast.place_ref, ...), custom_call_target="tpu_custom_call" | custom-call | flops 4831838208 | bytes 18950164 | tf_op jit(solution)/shard_map/student_attend/pallas_call | solution.py:411
  242.4 20.4 %student_hidden.1 = (bf16[4,768,768]{2,1,0:T(8,128)(2,1)}, bf16[4,512,768]{2,1,0:T(8,128)(2,1)}, bf16[4,768,512]{2,1,0:T(8,128)(2,1)}, bf16[4,512,768]{2,1,0:T(8,128)(2,1)}, bf16[4,512,768]{2,1,0:T(8,128)(2,1)}) custom-call(s32[1]{0:T(128)} %bitcast.place_ref, f32[4]{0:T(128)} %clips_ref.17, bf16[512,768]{1,0:T(8,128)(2,1)} %get-tuple-element.83.refs_0_, ...), custom_call_target="tpu_custom_call" | custom-call | flops 4831838208 | bytes 22806548 | tf_op jit(solution)/shard_map/student_hidden/pallas_call | solution.py:411
  264.2 10.8 %student_output.1 = (bf16[4,768,768]{2,1,0:T(8,128)(2,1)}, bf16[256,768]{1,0:T(8,128)(2,1)}, bf16[256,768]{1,0:T(8,128)(2,1)}, f32[512,768]{1,0:T(8,128)}, bf16[...) custom-call(s32[1]{0:T(128)} %bitcast.place_ref, bf16[4,512,768]{2,1,0:T(8,128)(2,1)} %get-tuple-element.84.refs_0_, ...), custom_call_target="tpu_custom_call" | custom-call | flops 2415919104 | bytes 19679236 | tf_op jit(solution)/shard_map/student_output/pallas_call | solution.py:411
  275.0 9.6 %hidden_back.1 = (bf16[4,512,768]{2,1,0:T(8,128)(2,1)}, f32[1,768]{1,0:T(1,128)}) custom-call(bf16[512,768]{1,0:T(8,128)(2,1)} %get-tuple-element.94.grad_low.right, bf16[4,768,768]{2,1,0:T(8,128)(2,1)} %get-tuple-element.95.full, bf16[4,512,768]{2,1,0:T(8,128)(2,1)} %get-tuple-element.96.slope, bf16[4,512,768]{2,1,0:T(8,128)(2,1)} %get-tuple-element.97.clip), custom_call_target="tpu_custom_call" | custom-call | flops 3019898880 | bytes 14945280 | tf_op jit(solution)/shard_map/hidden_back/pallas_call | solution.py:411
  284.6 11.1 %first_back.1 = (f32[512,768]{1,0:T(8,128)}, bf16[512,768]{1,0:T(8,128)(2,1)}, bf16[768,512]{1,0:T(8,128)(2,1)}, f32[1,768]{1,0:T(1,128)}, f32[1,768]{1,0:T(1,128)}, /*index=5*/f32[1,768]{1,0:T(1,128)}) custom-call(f32[4]{0:T(128)} %clips_ref.17, bf16[4,512,768]{2,1,0:T(8,128)(2,1)} %get-tuple-element.98.grad_hidden.right, ...), custom_call_target="tpu_custom_call" | custom-call | flops 2415919104 | bytes 14171152 | tf_op jit(solution)/shard_map/first_back/pallas_call | solution.py:411
  298.5 8.0 %ffn_out_weight.1 = (bf16[4,4,96,768]{3,2,1,0:T(8,128)(2,1)}, bf16[4,4,96,768]{3,2,1,0:T(8,128)(2,1)}) custom-call(s32[1]{0:T(128)} %bitcast.place_ref, bf16[4,768,512]{2,1,0:T(8,128)(2,1)} %get-tuple-element.122.left_t, bf16[512,768]{1,0:T(8,128)(2,1)} %get-tuple-element.94.grad_low.right), custom_call_target="tpu_custom_call" | custom-call | flops 2415919104 | bytes 8650756 | tf_op jit(solution)/shard_map/ffn_out_weight/pallas_call | solution.py:411
  306.5 9.1 %attend_back.4 = (bf16[4,1,96,768]{3,2,1,0:T(8,128)(2,1)}, bf16[4,1,96,768]{3,2,1,0:T(8,128)(2,1)}, f32[1,192]{1,0:T(1,128)}, f32[512,768]{1,0:T(8,128)}) custom-call(s32[1]{0:T(128)} %bitcast.place_ref, f32[4]{0:T(128)} %clips_ref.17, s32[1,512]{1,0:T(1,128)} %broadcast_select_fusion.1.refs_2_.refs_0_, s32[512,1]{1,0:T(8,128)} %broadcast_select_fusion.refs_3_.refs_1_, ...), custom_call_target="tpu_custom_call" | custom-call | flops 3019898880 | bytes 12582912 | tf_op jit(solution)/shard_map/attend_back/pallas_call | solution.py:756
  315.7 9.6 %attend_back.5 = (bf16[4,1,96,768]{3,2,1,0:T(8,128)(2,1)}, bf16[4,1,96,768]{3,2,1,0:T(8,128)(2,1)}, f32[1,192]{1,0:T(1,128)}, f32[512,768]{1,0:T(8,128)}) custom-call(s32[1]{0:T(128)} %bitcast.place_ref, f32[4]{0:T(128)} %clips_ref.17, s32[1,512]{1,0:T(1,128)} %broadcast_select_fusion.1.refs_2_.refs_0_, s32[512,1]{1,0:T(8,128)} %broadcast_select_fusion.refs_3_.refs_1_, ...), custom_call_target="tpu_custom_call" | custom-call | flops 3019898880 | bytes 12582912 | tf_op jit(solution)/shard_map/attend_back/pallas_call | solution.py:756
  326.9 9.8 %attend_back.6 = (bf16[4,1,96,768]{3,2,1,0:T(8,128)(2,1)}, bf16[4,1,96,768]{3,2,1,0:T(8,128)(2,1)}, f32[1,192]{1,0:T(1,128)}, f32[512,768]{1,0:T(8,128)}) custom-call(s32[1]{0:T(128)} %bitcast.place_ref, f32[4]{0:T(128)} %clips_ref.17, s32[1,512]{1,0:T(1,128)} %broadcast_select_fusion.1.refs_2_.refs_0_, s32[512,1]{1,0:T(8,128)} %broadcast_select_fusion.refs_3_.refs_1_, ...), custom_call_target="tpu_custom_call" | custom-call | flops 3019898880 | bytes 12582912 | tf_op jit(solution)/shard_map/attend_back/pallas_call | solution.py:756
  338.6 10.1 %attend_back.7 = (bf16[4,1,96,768]{3,2,1,0:T(8,128)(2,1)}, bf16[4,1,96,768]{3,2,1,0:T(8,128)(2,1)}, f32[1,192]{1,0:T(1,128)}, f32[256,768]{1,0:T(8,128)}, bf16[256,768]{1,0:T(8,128)(2,1)}, /*index=5*/f32[1,768]{1,0:T(1,128)}) custom-call(s32[1]{0:T(128)} %bitcast.place_ref, f32[4]{0:T(128)} %clips_ref.17, s32[1,512]{1,0:T(1,128)} %broadcast_select_fusion.1.refs_2_.refs_0_, ...), custom_call_target="tpu_custom_call" | custom-call | flops 3019898880 | bytes 12582912 | tf_op jit(solution)/shard_map/attend_back/pallas_call | solution.py:756
  349.1 7.9 %ffn_in_weight.1 = (bf16[4,4,96,768]{3,2,1,0:T(8,128)(2,1)}, bf16[4,4,96,768]{3,2,1,0:T(8,128)(2,1)}) custom-call(s32[1]{0:T(128)} %bitcast.place_ref, bf16[768,512]{1,0:T(8,128)(2,1)} %get-tuple-element.119.left_t, bf16[4,512,768]{2,1,0:T(8,128)(2,1)} %get-tuple-element.98.grad_hidden.right), custom_call_target="tpu_custom_call" | custom-call | flops 2415919104 | bytes 8650756 | tf_op jit(solution)/shard_map/ffn_in_weight/pallas_call | solution.py:411
  367.4 6.9 %collective-permute-done.72 = bf16[256,768]{1,0:T(8,128)(2,1)S(1)} collective-permute-done((bf16[256,768]{1,0:T(8,128)(2,1)}, bf16[256,768]{1,0:T(8,128)(2,1)S(1)}, u32[]{:S(2)}, u32[]{:S(2)}) %collective-permute-start.72) | collective-permute-done | bytes 393248 | tf_op jit(solution)/shard_map/ppermute | solution.py:429
  388.3 2.8 collective-permute-done.91
  394.7 3.0 collective-permute-done.87
  404.6 2.9 collective-permute-done.94
  409.4 3.5 collective-permute-start.83
  420.8 11.2 %collective-permute-done.111 = bf16[2,4,48,768]{3,2,1,0:T(8,128)(2,1)S(1)} collective-permute-done((bf16[2,4,48,768]{3,2,1,0:T(8,128)(2,1)S(1)}, bf16[2,4,48,768]{3,2,1,0:T(8,128)(2,1)S(1)}, u32[]{:S(2)}, u32[]{:S(2)}) %collective-permute-start.111) | collective-permute-done | bytes 589856 | tf_op jit(solution)/shard_map/ppermute | solution.py:429
  435.2 6.9 %collective-permute-done.103 = bf16[2,4,48,768]{3,2,1,0:T(8,128)(2,1)S(1)} collective-permute-done((bf16[2,4,48,768]{3,2,1,0:T(8,128)(2,1)S(1)}, bf16[2,4,48,768]{3,2,1,0:T(8,128)(2,1)S(1)}, u32[]{:S(2)}, u32[]{:S(2)}) %collective-permute-start.103) | collective-permute-done | bytes 589856 | tf_op jit(solution)/shard_map/ppermute | solution.py:429
  442.2 3.0 collective-permute-done.105
  452.2 2.8 collective-permute-done.106
  455.4 4.4 collective-permute-done.115
  462.0 6.8 %collective-permute-done.116 = bf16[96,768]{1,0:T(8,128)(2,1)S(1)} collective-permute-done((bf16[96,768]{1,0:T(8,128)(2,1)S(1)}, bf16[96,768]{1,0:T(8,128)(2,1)S(1)}, u32[]{:S(2)}, u32[]{:S(2)}) %collective-permute-start.116) | collective-permute-done | bytes 147488 | tf_op jit(solution)/shard_map/ppermute | solution.py:433
  471.3 3.4 collective-permute-start.108
  476.0 3.2 collective-permute-done.108
  482.4 3.9 concatenate.284
  501.2 3.2 collective-permute-done.122
  507.1 2.6 select_select_fusion
  527.6 3.5 finish.3
  531.1 3.6 slice_bitcast_fusion
  540.4 3.5 finish.4
  545.1 3.5 finish.5
  (634 shorter events, 232.7 us)
Async XLA Ops:
  2.4 72.6 %collective-permute-start.65 = (bf16[96,768]{1,0:T(8,128)(2,1)}, bf16[96,768]{1,0:T(8,128)(2,1)}, u32[]{:S(2)}, u32[]{:S(2)}) collective-permute-start(bf16[96,768]{1,0:T(8,128)(2,1)} %constant_dynamic-slice_fusion.1), channel_id=1, source_target_pairs={{0,3},{1,0},{2,1},{3,2},{4,7},{5,4},{6,5},{7,6},{8,11},{9,8},{10,9... | collective-permute-start | bytes 442376 | tf_op jit(solution)/shard_map/ppermute | solution.py:433
  7.4 48.3 %collective-permute-start.60 = (bf16[96,768]{1,0:T(8,128)(2,1)}, bf16[96,768]{1,0:T(8,128)(2,1)}, u32[]{:S(2)}, u32[]{:S(2)}) collective-permute-start(bf16[96,768]{1,0:T(8,128)(2,1)} %constant_dynamic-slice_fusion.1), channel_id=1, source_target_pairs={{0,2},{1,3},{2,0},{3,1},{4,6},{5,7},{6,4},{7,5},{8,10},{9,11},{10,... | collective-permute-start | bytes 442376 | tf_op jit(solution)/shard_map/ppermute | solution.py:433
  7.4 66.5 %collective-permute-start.59 = (bf16[96,768]{1,0:T(8,128)(2,1)}, bf16[96,768]{1,0:T(8,128)(2,1)}, u32[]{:S(2)}, u32[]{:S(2)}) collective-permute-start(bf16[96,768]{1,0:T(8,128)(2,1)} %constant_dynamic-slice_fusion.1), channel_id=1, source_target_pairs={{0,1},{1,2},{2,3},{3,0},{4,5},{5,6},{6,7},{7,4},{8,9},{9,10},{10,1... | collective-permute-start | bytes 442376 | tf_op jit(solution)/shard_map/ppermute | solution.py:433
  10.0 59.4 %collective-permute-start.54 = (bf16[96,768]{1,0:T(8,128)(2,1)}, bf16[96,768]{1,0:T(8,128)(2,1)}, u32[]{:S(2)}, u32[]{:S(2)}) collective-permute-start(bf16[96,768]{1,0:T(8,128)(2,1)} %constant_dynamic-slice_fusion.2), channel_id=1, source_target_pairs={{0,3},{1,0},{2,1},{3,2},{4,7},{5,4},{6,5},{7,6},{8,11},{9,8},{10,9... | collective-permute-start | bytes 442376 | tf_op jit(solution)/shard_map/ppermute | solution.py:433
  23.4 17.6 %collective-permute-start.1 = (f32[1,128]{1,0:T(1,128)}, f32[1,128]{1,0:T(1,128)}, u32[]{:S(2)}, u32[]{:S(2)}) collective-permute-start(f32[1,128]{1,0:T(1,128)} %fusion.87), channel_id=1, source_target_pairs={{0,1},{1,0},{2,3},{3,2},{4,5},{5,4},{6,7},{7,6},{8,9},{9,8},{10,11... | collective-permute-start | bytes 1544 | tf_op jit(solution)/shard_map/ppermute | solution.py:429
  69.4 31.0 %collective-permute-start.9 = (bf16[96,768]{1,0:T(8,128)(2,1)S(1)}, bf16[96,768]{1,0:T(8,128)(2,1)S(1)}, u32[]{:S(2)}, u32[]{:S(2)}) collective-permute-start(bf16[96,768]{1,0:T(8,128)(2,1)S(1)} %constant_dynamic-slice_fusion.6), channel_id=1, source_target_pairs={{0,3},{1,0},{2,1},{3,2},{4,7},{5,4},{6,5},{7,6},{8,11},{9,8},{10,9... | collective-permute-start | bytes 442376 | tf_op jit(solution)/shard_map/ppermute | solution.py:433
  75.0 25.3 %collective-permute-start.3 = (bf16[96,768]{1,0:T(8,128)(2,1)S(1)}, bf16[96,768]{1,0:T(8,128)(2,1)S(1)}, u32[]{:S(2)}, u32[]{:S(2)}) collective-permute-start(bf16[96,768]{1,0:T(8,128)(2,1)S(1)} %constant_dynamic-slice_fusion.6), channel_id=1, source_target_pairs={{0,1},{1,2},{2,3},{3,0},{4,5},{5,6},{6,7},{7,4},{8,9},{9,10},{10,1... | collective-permute-start | bytes 442376 | tf_op jit(solution)/shard_map/ppermute | solution.py:433
  77.8 25.7 %collective-permute-start.31 = (bf16[96,768]{1,0:T(8,128)(2,1)S(1)}, bf16[96,768]{1,0:T(8,128)(2,1)S(1)}, u32[]{:S(2)}, u32[]{:S(2)}) collective-permute-start(bf16[96,768]{1,0:T(8,128)(2,1)S(1)} %constant_dynamic-slice_fusion.4), channel_id=1, source_target_pairs={{0,3},{1,0},{2,1},{3,2},{4,7},{5,4},{6,5},{7,6},{8,11},{9,8},{10,9... | collective-permute-start | bytes 442376 | tf_op jit(solution)/shard_map/ppermute | solution.py:433
  79.9 19.8 %collective-permute-start.26 = (bf16[96,768]{1,0:T(8,128)(2,1)S(1)}, bf16[96,768]{1,0:T(8,128)(2,1)S(1)}, u32[]{:S(2)}, u32[]{:S(2)}) collective-permute-start(bf16[96,768]{1,0:T(8,128)(2,1)S(1)} %constant_dynamic-slice_fusion.4), channel_id=1, source_target_pairs={{0,2},{1,3},{2,0},{3,1},{4,6},{5,7},{6,4},{7,5},{8,10},{9,11},{10,... | collective-permute-start | bytes 442376 | tf_op jit(solution)/shard_map/ppermute | solution.py:433
  125.1 18.0 %collective-permute-start = (bf16[256,768]{1,0:T(8,128)(2,1)S(1)}, bf16[256,768]{1,0:T(8,128)(2,1)S(1)}, u32[]{:S(2)}, u32[]{:S(2)}) collective-permute-start(bf16[256,768]{1,0:T(8,128)(2,1)S(1)} %copy-done.56), channel_id=1, source_target_pairs={{0,1},{1,0},{2,3},{3,2},{4,5},{5,4},{6,7},{7,6},{8,9},{9,8},{10,11... | collective-permute-start | bytes 1179656 | tf_op jit(solution)/shard_map/ppermute | solution.py:429
  126.5 18.2 %collective-permute-start.36 = (bf16[256,768]{1,0:T(8,128)(2,1)S(1)}, bf16[256,768]{1,0:T(8,128)(2,1)}, u32[]{:S(2)}, u32[]{:S(2)}) collective-permute-start(bf16[256,768]{1,0:T(8,128)(2,1)S(1)} %copy-done.55), channel_id=1, source_target_pairs={{0,1},{1,0},{2,3},{3,2},{4,5},{5,4},{6,7},{7,6},{8,9},{9,8},{10,11... | collective-permute-start | bytes 1179656 | tf_op jit(solution)/shard_map/ppermute | solution.py:429
  148.1 17.6 %collective-permute-start.67 = (bf16[288,768]{1,0:T(8,128)(2,1)S(1)}, bf16[288,768]{1,0:T(8,128)(2,1)}, u32[]{:S(2)}, u32[]{:S(2)}) collective-permute-start(bf16[288,768]{1,0:T(8,128)(2,1)S(1)} %pad_maximum_fusion.20.refs_8_), channel_id=1, source_target_pairs={{0,8},{4,12},{8,0},{12,4},{16,24},{20,28},{24,16},{28,20},{1,9},{5... | collective-permute-start | bytes 1327112 | tf_op jit(solution)/shard_map/ppermute | solution.py:429
  175.4 22.1 %collective-permute-start.11 = (bf16[288,768]{1,0:T(8,128)(2,1)S(1)}, bf16[288,768]{1,0:T(8,128)(2,1)S(1)}, u32[]{:S(2)}, u32[]{:S(2)}) collective-permute-start(bf16[288,768]{1,0:T(8,128)(2,1)S(1)} %pad_maximum_fusion.10.refs_11_), channel_id=1, source_target_pairs={{0,8},{4,12},{8,0},{12,4},{16,24},{20,28},{24,16},{28,20},{1,9},{5... | collective-permute-start | bytes 1327112 | tf_op jit(solution)/shard_map/ppermute | solution.py:429
  179.1 20.3 %collective-permute-start.53 = (bf16[288,768]{1,0:T(8,128)(2,1)}, bf16[288,768]{1,0:T(8,128)(2,1)}, u32[]{:S(2)}, u32[]{:S(2)}) collective-permute-start(bf16[288,768]{1,0:T(8,128)(2,1)} %collective-permute-done.51.refs_3_), channel_id=1, source_target_pairs={{0,4},{4,0},{8,12},{12,8},{16,20},{20,16},{24,28},{28,24},{1,5},{5... | collective-permute-start | bytes 1327112 | tf_op jit(solution)/shard_map/ppermute | solution.py:429
  179.1 20.5 %collective-permute-start.58 = (bf16[288,768]{1,0:T(8,128)(2,1)}, bf16[288,768]{1,0:T(8,128)(2,1)}, u32[]{:S(2)}, u32[]{:S(2)}) collective-permute-start(bf16[288,768]{1,0:T(8,128)(2,1)} %collective-permute-done.56.refs_7_), channel_id=1, source_target_pairs={{0,4},{4,0},{8,12},{12,8},{16,20},{20,16},{24,28},{28,24},{1,5},{5... | collective-permute-start | bytes 1327112 | tf_op jit(solution)/shard_map/ppermute | solution.py:429
  179.6 21.5 %collective-permute-start.64 = (bf16[288,768]{1,0:T(8,128)(2,1)S(1)}, bf16[288,768]{1,0:T(8,128)(2,1)S(1)}, u32[]{:S(2)}, u32[]{:S(2)}) collective-permute-start(bf16[288,768]{1,0:T(8,128)(2,1)S(1)} %collective-permute-done.62.refs_5_), channel_id=1, source_target_pairs={{0,4},{4,0},{8,12},{12,8},{16,20},{20,16},{24,28},{28,24},{1,5},{5... | collective-permute-start | bytes 1327112 | tf_op jit(solution)/shard_map/ppermute | solution.py:429
  179.8 21.4 %collective-permute-start.69 = (bf16[288,768]{1,0:T(8,128)(2,1)}, bf16[288,768]{1,0:T(8,128)(2,1)S(1)}, u32[]{:S(2)}, u32[]{:S(2)}) collective-permute-start(bf16[288,768]{1,0:T(8,128)(2,1)} %collective-permute-done.67.refs_9_), channel_id=1, source_target_pairs={{0,4},{4,0},{8,12},{12,8},{16,20},{20,16},{24,28},{28,24},{1,5},{5... | collective-permute-start | bytes 1327112 | tf_op jit(solution)/shard_map/ppermute | solution.py:429
  197.5 23.4 %collective-permute-start.28 = (bf16[288,768]{1,0:T(8,128)(2,1)S(1)}, bf16[288,768]{1,0:T(8,128)(2,1)S(1)}, u32[]{:S(2)}, u32[]{:S(2)}) collective-permute-start(bf16[288,768]{1,0:T(8,128)(2,1)S(1)} %pad_maximum_fusion.13.refs_4_), channel_id=1, source_target_pairs={{0,16},{4,20},{8,24},{12,28},{16,0},{20,4},{24,8},{28,12},{1,17},{... | collective-permute-start | bytes 1327112 | tf_op jit(solution)/shard_map/ppermute | solution.py:429
  199.3 21.8 %collective-permute-start.17 = (bf16[288,768]{1,0:T(8,128)(2,1)S(1)}, bf16[288,768]{1,0:T(8,128)(2,1)}, u32[]{:S(2)}, u32[]{:S(2)}) collective-permute-start(bf16[288,768]{1,0:T(8,128)(2,1)S(1)} %pad_maximum_fusion.11.refs_2_), channel_id=1, source_target_pairs={{0,16},{4,20},{8,24},{12,28},{16,0},{20,4},{24,8},{28,12},{1,17},{... | collective-permute-start | bytes 1327112 | tf_op jit(solution)/shard_map/ppermute | solution.py:429
  199.6 21.9 %collective-permute-start.22 = (bf16[288,768]{1,0:T(8,128)(2,1)S(1)}, bf16[288,768]{1,0:T(8,128)(2,1)}, u32[]{:S(2)}, u32[]{:S(2)}) collective-permute-start(bf16[288,768]{1,0:T(8,128)(2,1)S(1)} %pad_maximum_fusion.12.refs_6_), channel_id=1, source_target_pairs={{0,8},{4,12},{8,0},{12,4},{16,24},{20,28},{24,16},{28,20},{1,9},{5... | collective-permute-start | bytes 1327112 | tf_op jit(solution)/shard_map/ppermute | solution.py:429
  201.1 21.0 %collective-permute-start.8 = (bf16[288,768]{1,0:T(8,128)(2,1)S(1)}, bf16[288,768]{1,0:T(8,128)(2,1)}, u32[]{:S(2)}, u32[]{:S(2)}) collective-permute-start(bf16[288,768]{1,0:T(8,128)(2,1)S(1)} %copy-done.89), channel_id=1, source_target_pairs={{0,4},{4,0},{8,12},{12,8},{16,20},{20,16},{24,28},{28,24},{1,5},{5... | collective-permute-start | bytes 1327112 | tf_op jit(solution)/shard_map/ppermute | solution.py:429
  201.2 20.9 %collective-permute-start.13 = (bf16[288,768]{1,0:T(8,128)(2,1)S(1)}, bf16[288,768]{1,0:T(8,128)(2,1)}, u32[]{:S(2)}, u32[]{:S(2)}) collective-permute-start(bf16[288,768]{1,0:T(8,128)(2,1)S(1)} %collective-permute-done.11.refs_12_), channel_id=1, source_target_pairs={{0,4},{4,0},{8,12},{12,8},{16,20},{20,16},{24,28},{28,24},{1,5},{5... | collective-permute-start | bytes 1327112 | tf_op jit(solution)/shard_map/ppermute | solution.py:429
  220.9 19.3 %collective-permute-start.18 = (bf16[288,768]{1,0:T(8,128)(2,1)S(1)}, bf16[288,768]{1,0:T(8,128)(2,1)S(1)}, u32[]{:S(2)}, u32[]{:S(2)}) collective-permute-start(bf16[288,768]{1,0:T(8,128)(2,1)S(1)} %pad_maximum_fusion.11.refs_2_), channel_id=1, source_target_pairs={{0,4},{4,0},{8,12},{12,8},{16,20},{20,16},{24,28},{28,24},{1,5},{5... | collective-permute-start | bytes 1327112 | tf_op jit(solution)/shard_map/ppermute | solution.py:429
  221.2 19.2 %collective-permute-start.23 = (bf16[288,768]{1,0:T(8,128)(2,1)S(1)}, bf16[288,768]{1,0:T(8,128)(2,1)S(1)}, u32[]{:S(2)}, u32[]{:S(2)}) collective-permute-start(bf16[288,768]{1,0:T(8,128)(2,1)S(1)} %pad_maximum_fusion.12.refs_6_), channel_id=1, source_target_pairs={{0,4},{4,0},{8,12},{12,8},{16,20},{20,16},{24,28},{28,24},{1,5},{5... | collective-permute-start | bytes 1327112 | tf_op jit(solution)/shard_map/ppermute | solution.py:429
  221.5 18.6 %collective-permute-start.33 = (bf16[288,768]{1,0:T(8,128)(2,1)S(1)}, bf16[288,768]{1,0:T(8,128)(2,1)S(1)}, u32[]{:S(2)}, u32[]{:S(2)}) collective-permute-start(bf16[288,768]{1,0:T(8,128)(2,1)S(1)} %pad_maximum_fusion.14.refs_8_), channel_id=1, source_target_pairs={{0,8},{4,12},{8,0},{12,4},{16,24},{20,28},{24,16},{28,20},{1,9},{5... | collective-permute-start | bytes 1327112 | tf_op jit(solution)/shard_map/ppermute | solution.py:429
  222.1 19.2 %collective-permute-start.19 = (bf16[288,768]{1,0:T(8,128)(2,1)}, bf16[288,768]{1,0:T(8,128)(2,1)S(1)}, u32[]{:S(2)}, u32[]{:S(2)}) collective-permute-start(bf16[288,768]{1,0:T(8,128)(2,1)} %collective-permute-done.17.refs_3_), channel_id=1, source_target_pairs={{0,4},{4,0},{8,12},{12,8},{16,20},{20,16},{24,28},{28,24},{1,5},{5... | collective-permute-start | bytes 1327112 | tf_op jit(solution)/shard_map/ppermute | solution.py:429
  222.1 19.9 %collective-permute-start.24 = (bf16[288,768]{1,0:T(8,128)(2,1)}, bf16[288,768]{1,0:T(8,128)(2,1)}, u32[]{:S(2)}, u32[]{:S(2)}) collective-permute-start(bf16[288,768]{1,0:T(8,128)(2,1)} %collective-permute-done.22.refs_7_), channel_id=1, source_target_pairs={{0,4},{4,0},{8,12},{12,8},{16,20},{20,16},{24,28},{28,24},{1,5},{5... | collective-permute-start | bytes 1327112 | tf_op jit(solution)/shard_map/ppermute | solution.py:429
  240.1 22.7 %collective-permute-start.70 = (bf16[256,768]{1,0:T(8,128)(2,1)S(1)}, bf16[256,768]{1,0:T(8,128)(2,1)S(1)}, u32[]{:S(2)}, u32[]{:S(2)}) collective-permute-start(bf16[256,768]{1,0:T(8,128)(2,1)S(1)} %copy-done.54), channel_id=1, source_target_pairs={{0,1},{1,0},{2,3},{3,2},{4,5},{5,4},{6,7},{7,6},{8,9},{9,8},{10,11... | collective-permute-start | bytes 1179656 | tf_op jit(solution)/shard_map/ppermute | solution.py:429
  240.3 22.6 %collective-permute-start.29 = (bf16[288,768]{1,0:T(8,128)(2,1)S(1)}, bf16[288,768]{1,0:T(8,128)(2,1)S(1)}, u32[]{:S(2)}, u32[]{:S(2)}) collective-permute-start(bf16[288,768]{1,0:T(8,128)(2,1)S(1)} %pad_maximum_fusion.13.refs_4_), channel_id=1, source_target_pairs={{0,4},{4,0},{8,12},{12,8},{16,20},{20,16},{24,28},{28,24},{1,5},{5... | collective-permute-start | bytes 1327112 | tf_op jit(solution)/shard_map/ppermute | solution.py:429
  240.4 22.5 %collective-permute-start.34 = (bf16[288,768]{1,0:T(8,128)(2,1)S(1)}, bf16[288,768]{1,0:T(8,128)(2,1)S(1)}, u32[]{:S(2)}, u32[]{:S(2)}) collective-permute-start(bf16[288,768]{1,0:T(8,128)(2,1)S(1)} %pad_maximum_fusion.14.refs_8_), channel_id=1, source_target_pairs={{0,4},{4,0},{8,12},{12,8},{16,20},{20,16},{24,28},{28,24},{1,5},{5... | collective-permute-start | bytes 1327112 | tf_op jit(solution)/shard_map/ppermute | solution.py:429
  241.2 21.6 %collective-permute-start.30 = (bf16[288,768]{1,0:T(8,128)(2,1)S(1)}, bf16[288,768]{1,0:T(8,128)(2,1)S(1)}, u32[]{:S(2)}, u32[]{:S(2)}) collective-permute-start(bf16[288,768]{1,0:T(8,128)(2,1)S(1)} %collective-permute-done.28.refs_5_), channel_id=1, source_target_pairs={{0,4},{4,0},{8,12},{12,8},{16,20},{20,16},{24,28},{28,24},{1,5},{5... | collective-permute-start | bytes 1327112 | tf_op jit(solution)/shard_map/ppermute | solution.py:429
  242.0 20.9 %collective-permute-start.35 = (bf16[288,768]{1,0:T(8,128)(2,1)S(1)}, bf16[288,768]{1,0:T(8,128)(2,1)S(1)}, u32[]{:S(2)}, u32[]{:S(2)}) collective-permute-start(bf16[288,768]{1,0:T(8,128)(2,1)S(1)} %collective-permute-done.33.refs_9_), channel_id=1, source_target_pairs={{0,4},{4,0},{8,12},{12,8},{16,20},{20,16},{24,28},{28,24},{1,5},{5... | collective-permute-start | bytes 1327112 | tf_op jit(solution)/shard_map/ppermute | solution.py:429
  296.4 28.9 %collective-permute-start.135 = (f32[4,768]{1,0:T(4,128)S(1)}, f32[4,768]{1,0:T(4,128)S(1)}, u32[]{:S(2)}, u32[]{:S(2)}) collective-permute-start(f32[4,768]{1,0:T(4,128)S(1)} %pad_maximum_fusion.52), channel_id=1, source_target_pairs={{0,4},{4,0},{8,12},{12,8},{16,20},{20,16},{24,28},{28,24},{1,5},{5... | collective-permute-start | bytes 36872 | tf_op jit(solution)/shard_map/ppermute | solution.py:429
  296.6 68.7 %collective-permute-start.71 = (bf16[256,768]{1,0:T(8,128)(2,1)}, bf16[256,768]{1,0:T(8,128)(2,1)}, u32[]{:S(2)}, u32[]{:S(2)}) collective-permute-start(bf16[256,768]{1,0:T(8,128)(2,1)} %get-tuple-element.89), channel_id=1, source_target_pairs={{0,1},{1,0},{2,3},{3,2},{4,5},{5,4},{6,7},{7,6},{8,9},{9,8},{10,11... | collective-permute-start | bytes 1179656 | tf_op jit(solution)/shard_map/ppermute | solution.py:429
  315.6 60.0 %collective-permute-start.73 = (bf16[4,1,96,768]{3,2,1,0:T(8,128)(2,1)}, bf16[4,1,96,768]{3,2,1,0:T(8,128)(2,1)}, u32[]{:S(2)}, u32[]{:S(2)}) collective-permute-start(bf16[4,1,96,768]{3,2,1,0:T(8,128)(2,1)} %get-tuple-element.112), channel_id=1, source_target_pairs={{0,4},{4,0},{8,12},{12,8},{16,20},{20,16},{24,28},{28,24},{1,5},{5... | collective-permute-start | bytes 1769480 | tf_op jit(solution)/shard_map/ppermute | solution.py:429
  361.2 51.7 %collective-permute-start.110 = (bf16[4,4,96,768]{3,2,1,0:T(8,128)(2,1)}, bf16[4,4,96,768]{3,2,1,0:T(8,128)(2,1)}, u32[]{:S(2)}, u32[]{:S(2)}) collective-permute-start(bf16[4,4,96,768]{3,2,1,0:T(8,128)(2,1)} %get-tuple-element.124), channel_id=1, source_target_pairs={{0,4},{4,0},{8,12},{12,8},{16,20},{20,16},{24,28},{28,24},{1,5},{5... | collective-permute-start | bytes 7077896 | tf_op jit(solution)/shard_map/ppermute | solution.py:429
  384.3 32.5 %collective-permute-start.102 = (bf16[4,4,96,768]{3,2,1,0:T(8,128)(2,1)S(1)}, bf16[4,4,96,768]{3,2,1,0:T(8,128)(2,1)S(1)}, u32[]{:S(2)}, u32[]{:S(2)}) collective-permute-start(bf16[4,4,96,768]{3,2,1,0:T(8,128)(2,1)S(1)} %copy-done.84), channel_id=1, source_target_pairs={{0,4},{4,0},{8,12},{12,8},{16,20},{20,16},{24,28},{28,24},{1,5},{5... | collective-permute-start | bytes 7077896 | tf_op jit(solution)/shard_map/ppermute | solution.py:429
  392.0 16.5 %collective-permute-start.75 = (bf16[1,48,768]{2,1,0:T(8,128)(2,1)S(1)}, bf16[1,48,768]{2,1,0:T(8,128)(2,1)S(1)}, u32[]{:S(2)}, u32[]{:S(2)}) collective-permute-start(bf16[1,48,768]{2,1,0:T(8,128)(2,1)S(1)} %get-tuple-element.202), channel_id=1, source_target_pairs={{0,16},{4,20},{8,24},{12,28},{16,0},{20,4},{24,8},{28,12},{1,17},{... | collective-permute-start | bytes 221192 | tf_op jit(solution)/shard_map/ppermute | solution.py:429
  409.4 61.9 %collective-permute-start.83 = (bf16[96,768]{1,0:T(8,128)(2,1)S(1)}, bf16[96,768]{1,0:T(8,128)(2,1)S(1)}, u32[]{:S(2)}, u32[]{:S(2)}) collective-permute-start(bf16[96,768]{1,0:T(8,128)(2,1)S(1)} %maximum_bitcast_fusion.1), channel_id=1, source_target_pairs={{0,3},{1,0},{2,1},{3,2},{4,7},{5,4},{6,5},{7,6},{8,11},{9,8},{10,9... | collective-permute-start | bytes 442376 | tf_op jit(solution)/shard_map/ppermute | solution.py:433
  418.9 23.2 %collective-permute-start.103 = (bf16[2,4,48,768]{3,2,1,0:T(8,128)(2,1)S(1)}, bf16[2,4,48,768]{3,2,1,0:T(8,128)(2,1)S(1)}, u32[]{:S(2)}, u32[]{:S(2)}) collective-permute-start(bf16[2,4,48,768]{3,2,1,0:T(8,128)(2,1)S(1)} %pad_maximum_fusion.7), channel_id=1, source_target_pairs={{0,8},{4,12},{8,0},{12,4},{16,24},{20,28},{24,16},{28,20},{1,9},{5... | collective-permute-start | bytes 1769480 | tf_op jit(solution)/shard_map/ppermute | solution.py:429
  419.5 25.6 %collective-permute-start.105 = (bf16[2,4,48,768]{3,2,1,0:T(8,128)(2,1)S(1)}, bf16[2,4,48,768]{3,2,1,0:T(8,128)(2,1)S(1)}, u32[]{:S(2)}, u32[]{:S(2)}) collective-permute-start(bf16[2,4,48,768]{3,2,1,0:T(8,128)(2,1)S(1)} %stack.118), channel_id=1, source_target_pairs={{0,16},{4,20},{8,24},{12,28},{16,0},{20,4},{24,8},{28,12},{1,17},{... | collective-permute-start | bytes 1769480 | tf_op jit(solution)/shard_map/ppermute | solution.py:429
  442.1 34.0 %collective-permute-start.95 = (bf16[96,768]{1,0:T(8,128)(2,1)S(1)}, bf16[96,768]{1,0:T(8,128)(2,1)S(1)}, u32[]{:S(2)}, u32[]{:S(2)}) collective-permute-start(bf16[96,768]{1,0:T(8,128)(2,1)S(1)} %maximum_bitcast_fusion.3), channel_id=1, source_target_pairs={{0,1},{1,2},{2,3},{3,0},{4,5},{5,6},{6,7},{7,4},{8,9},{9,10},{10,1... | collective-permute-start | bytes 442376 | tf_op jit(solution)/shard_map/ppermute | solution.py:433
  493.9 17.0 %collective-permute-start.129 = (bf16[48,768]{1,0:T(8,128)(2,1)S(1)}, bf16[48,768]{1,0:T(8,128)(2,1)S(1)}, u32[]{:S(2)}, u32[]{:S(2)}) collective-permute-start(bf16[48,768]{1,0:T(8,128)(2,1)S(1)} %get-tuple-element.254), channel_id=1, source_target_pairs={{0,8},{4,12},{8,0},{12,4},{16,24},{20,28},{24,16},{28,20},{1,9},{5... | collective-permute-start | bytes 221192 | tf_op jit(solution)/shard_map/ppermute | solution.py:429
  494.4 16.7 %collective-permute-start.130 = (bf16[48,768]{1,0:T(8,128)(2,1)S(1)}, bf16[48,768]{1,0:T(8,128)(2,1)S(1)}, u32[]{:S(2)}, u32[]{:S(2)}) collective-permute-start(bf16[48,768]{1,0:T(8,128)(2,1)S(1)} %get-tuple-element.255), channel_id=1, source_target_pairs={{0,16},{4,20},{8,24},{12,28},{16,0},{20,4},{24,8},{28,12},{1,17},{... | collective-permute-start | bytes 221192 | tf_op jit(solution)/shard_map/ppermute | solution.py:429
  496.5 20.9 %collective-permute-start.123 = (bf16[48,768]{1,0:T(8,128)(2,1)S(1)}, bf16[48,768]{1,0:T(8,128)(2,1)S(1)}, u32[]{:S(2)}, u32[]{:S(2)}) collective-permute-start(bf16[48,768]{1,0:T(8,128)(2,1)S(1)} %get-tuple-element.256), channel_id=1, source_target_pairs={{0,8},{4,12},{8,0},{12,4},{16,24},{20,28},{24,16},{28,20},{1,9},{5... | collective-permute-start | bytes 221192 | tf_op jit(solution)/shard_map/ppermute | solution.py:429
  498.0 20.3 %collective-permute-start.124 = (bf16[48,768]{1,0:T(8,128)(2,1)S(1)}, bf16[48,768]{1,0:T(8,128)(2,1)S(1)}, u32[]{:S(2)}, u32[]{:S(2)}) collective-permute-start(bf16[48,768]{1,0:T(8,128)(2,1)S(1)} %get-tuple-element.257), channel_id=1, source_target_pairs={{0,16},{4,20},{8,24},{12,28},{16,0},{20,4},{24,8},{28,12},{1,17},{... | collective-permute-start | bytes 221192 | tf_op jit(solution)/shard_map/ppermute | solution.py:429
  522.5 21.4 %collective-permute-start.133 = (bf16[192,768]{1,0:T(8,128)(2,1)}, bf16[192,768]{1,0:T(8,128)(2,1)}, u32[]{:S(2)}, u32[]{:S(2)}) collective-permute-start(bf16[192,768]{1,0:T(8,128)(2,1)} %pad_maximum_fusion.25), channel_id=1, source_target_pairs={{0,4},{4,0},{8,12},{12,8},{16,20},{20,16},{24,28},{28,24},{1,5},{5... | collective-permute-start | bytes 884744 | tf_op jit(solution)/shard_map/ppermute | solution.py:429
  524.8 19.1 %collective-permute-start.134 = (bf16[192,768]{1,0:T(8,128)(2,1)}, bf16[192,768]{1,0:T(8,128)(2,1)}, u32[]{:S(2)}, u32[]{:S(2)}) collective-permute-start(bf16[192,768]{1,0:T(8,128)(2,1)} %pad_maximum_fusion.26), channel_id=1, source_target_pairs={{0,4},{4,0},{8,12},{12,8},{16,20},{20,16},{24,28},{28,24},{1,5},{5... | collective-permute-start | bytes 884744 | tf_op jit(solution)/shard_map/ppermute | solution.py:429
  (192 other events, 2507.1 us)
